TPU v7x, 32 devices: a whole 2x2x4 slice. The times are simulated.
32 devices in a mesh: dp: 16 (over z, x, core), expert: 2 (over y).
Axes of the slice: x: 2, y: 2, z: 4, core: 2. Of those that a mesh axis runs over, the one named last changes fastest.
Arguments:
- tokens: bfloat16 [4096, 4096], P(('dp', 'expert')), may hold values from -6 to 6
- cotangent: bfloat16 [4096, 4096], P(('dp', 'expert')), may hold values from -1.1953125 to 1.1953125
- expert_ids: int32 [4096, 2], P(('dp', 'expert')), may hold values from 0 to 63, as said below
- gate_probs: bfloat16 [4096, 2], P(('dp', 'expert')), may hold values from 0.049804688 to 1
- gate_w: bfloat16 [2, 7168, 4096], P('expert', 'dp'), may hold values from -0.09375 to 0.09375
- up_w: bfloat16 [2, 7168, 4096], P('expert', 'dp'), may hold values from -0.09375 to 0.09375
- down_w: bfloat16 [2, 7168, 4096], P('expert', 'dp'), may hold values from -0.0625 to 0.0625
Outputs:
- grad_gate: bfloat16 [2, 7168, 4096], P('expert', 'dp')
- grad_up: bfloat16 [2, 7168, 4096], P('expert', 'dp')
- grad_down: bfloat16 [2, 7168, 4096], P('expert', 'dp')
- grad_probs: float32 [4096, 2], P(('dp', 'expert'))
Inputs may be any that keep to these rules, and one draw needn't show every extreme that they name: `expert_ids`: each token names two different experts. Split the rows into aligned blocks of 128 (the rows of one device) and those into aligned runs of 2 blocks: a block names any one expert below 2 at most 4 times, and a run names it at most 4 times; in every draw some block reaches 4 and some run reaches 4.
All inputs are finite; a program needn't handle non-finite values.
Results may differ from a plain program's by a relative error of at most 0.015.
Values may be sent and summed in bfloat16 or wider, within the bound.
A program may use at most 128 MiB of HBM per device.

v0:
```python
import jax
import jax.numpy as jnp
from jax import lax
from jax.sharding import PartitionSpec as P

ROW_CAPACITY = 4


def contract_rows(left, right):
    return lax.dot_general(
        left, right, (((0,), (0,)), ((), ())), preferred_element_type=jnp.float32
    )


def contract_cols(left, right):
    return lax.dot_general(
        left, right, (((1,), (1,)), ((), ())), preferred_element_type=jnp.float32
    )


def shards(tokens, cotangent, expert_ids, gate_probs, gate_w, up_w, down_w):
    owners = lax.axis_size("expert")
    slots = owners * ROW_CAPACITY
    flat_ids = expert_ids.reshape(-1)
    marks = (flat_ids[:, None] == jnp.arange(owners, dtype=jnp.int32)[None, :]).astype(jnp.int32)
    before = jnp.cumsum(marks, axis=0) - marks
    ranking = jnp.sum(before * marks, axis=1)
    target = jnp.where(jnp.sum(marks, axis=1) > 0, flat_ids * ROW_CAPACITY + ranking, -1)
    routing = (target[None, :] == jnp.arange(slots, dtype=jnp.int32)[:, None]).astype(jnp.float32)
    per_token = routing.reshape(slots, -1, 2).sum(axis=2).astype(jnp.bfloat16)
    send_x = jnp.dot(per_token, tokens, preferred_element_type=jnp.float32).astype(jnp.bfloat16)
    send_dy = jnp.dot(per_token, cotangent, preferred_element_type=jnp.float32).astype(jnp.bfloat16)
    send_p = jnp.dot(
        routing.astype(jnp.bfloat16), gate_probs.reshape(-1), preferred_element_type=jnp.float32
    ).astype(jnp.bfloat16)
    got_x, got_dy, got_p = (
        lax.all_to_all(
            send_x.reshape(owners, ROW_CAPACITY, -1),
            "expert",
            split_axis=0,
            concat_axis=0,
            tiled=True,
        ),
        lax.all_to_all(
            send_dy.reshape(owners, ROW_CAPACITY, -1),
            "expert",
            split_axis=0,
            concat_axis=0,
            tiled=True,
        ),
        lax.all_to_all(
            send_p.reshape(owners, ROW_CAPACITY), "expert", split_axis=0, concat_axis=0, tiled=True
        ),
    )
    rows_x = got_x.reshape(slots, -1)
    rows_dy = got_dy.reshape(slots, -1)
    rows_p = got_p.reshape(slots)
    gate_local = gate_w[0]
    up_local = up_w[0]
    down_local = down_w[0]
    piece_x = lax.all_gather(rows_x, "dp", axis=0, tiled=True)
    piece_dy = lax.all_gather(rows_dy, "dp", axis=0, tiled=True)
    piece_p = lax.all_gather(rows_p, "dp", axis=0, tiled=True)
    weight_p = piece_p.astype(jnp.float32)[:, None]
    gate_pre = contract_cols(piece_x, gate_local)
    up_pre = contract_cols(piece_x, up_local)
    sigma = jax.nn.sigmoid(gate_pre)
    hidden = (gate_pre * sigma * up_pre).astype(jnp.bfloat16)
    pulled = contract_cols(piece_dy, down_local)
    router = jnp.sum(hidden.astype(jnp.float32) * pulled, axis=1)
    scaled_dy = (weight_p * piece_dy.astype(jnp.float32)).astype(jnp.bfloat16)
    d_hidden = weight_p * pulled
    d_gate = (d_hidden * up_pre * sigma * (1.0 + gate_pre * (1.0 - sigma))).astype(jnp.bfloat16)
    d_up = (d_hidden * gate_pre * sigma).astype(jnp.bfloat16)
    new_gate = contract_rows(d_gate, piece_x)
    new_up = contract_rows(d_up, piece_x)
    new_down = contract_rows(hidden, scaled_dy)
    router_rows = lax.psum_scatter(router, "dp", scatter_dimension=0, tiled=True)
    returned = lax.all_to_all(
        router_rows.reshape(owners, ROW_CAPACITY), "expert", split_axis=0, concat_axis=0, tiled=True
    )
    grad_flat = jnp.dot(returned.reshape(slots), routing, precision=lax.Precision.HIGHEST)
    grad_gate = new_gate.astype(jnp.bfloat16)[None]
    grad_up = new_up.astype(jnp.bfloat16)[None]
    grad_down = new_down.astype(jnp.bfloat16)[None]
    return (grad_gate, grad_up, grad_down, grad_flat.reshape(-1, 2))


def solution(mesh):
    in_specs = (
        P(("dp", "expert"), None),
        P(("dp", "expert"), None),
        P(("dp", "expert"), None),
        P(("dp", "expert"), None),
        P("expert", "dp", None),
        P("expert", "dp", None),
        P("expert", "dp", None),
    )
    out_specs = (
        P("expert", "dp", None),
        P("expert", "dp", None),
        P("expert", "dp", None),
        P(("dp", "expert"), None),
    )
    return jax.shard_map(shards, mesh=mesh, in_specs=in_specs, out_specs=out_specs, check_vma=False)
```

profile of v0, /device:TPU:0, one launch (start us, length us, event | category | flops | bytes accessed | tf_op | source)
XLA Modules:
  0.0 154.8 jit_solution(6346251373040510375)
XLA Ops:
  7.2 0.9 copy.44
  8.4 0.6 reduce-window.6
  9.0 0.2 slice_reduce_fusion
  9.2 0.2 reduce-window.9
  9.7 0.2 gt.17
  10.0 0.7 add_select_fusion
  10.7 0.2 convolution_convert_fusion.3
  11.0 8.2 %all_to_all.29 = bf16[2,4,4096]{2,1,0:T(4,128)(2,1)S(1)} all-to-all(bf16[2,4,4096]{2,1,0:T(4,128)(2,1)S(1)} %reshape.108), channel_id=1, replica_groups=mesh['dp'=16,'expert'=2] {'expert'}, dimensions={0} | all-to-all | bytes 131072 | tf_op jit(solution)/shard_map/all_to_all | solution.py:37
  19.2 0.7 reshape.109
  19.9 1.5 convolution_convert_fusion.4
  21.4 6.5 %all_to_all.30 = bf16[2,4,4096]{2,1,0:T(4,128)(2,1)S(1)} all-to-all(bf16[2,4,4096]{2,1,0:T(4,128)(2,1)S(1)} %reshape.106), channel_id=1, replica_groups=mesh['dp'=16,'expert'=2] {'expert'}, dimensions={0} | all-to-all | bytes 131072 | tf_op jit(solution)/shard_map/all_to_all | solution.py:44
  27.9 0.7 reshape.107
  28.6 0.8 copy.46
  29.6 0.7 all_to_all.24
  30.3 3.2 %all-to-all-start = ((bf16[2,1,4]{2,1,0:T(2,128)(2,1)}), bf16[2,1,4]{2,1,0:T(2,128)(2,1)S(1)}, u32[]{:S(2)}, u32[]{:S(2)}) async-start(bf16[2,1,4]{2,1,0:T(2,128)(2,1)} %all_to_all.24), calls=%async_computation | async-start | bytes 2048 | tf_op jit(solution)/shard_map/all_to_all | solution.py:51
  33.5 0.6 fusion.26
  35.4 1.8 %all-to-all-done = bf16[2,1,4]{2,1,0:T(2,128)(2,1)S(1)} async-done(((bf16[2,1,4]{2,1,0:T(2,128)(2,1)}), bf16[2,1,4]{2,1,0:T(2,128)(2,1)S(1)}, u32[]{:S(2)}, u32[]{:S(2)}) %all-to-all-start) | async-done | bytes 48 | tf_op jit(solution)/shard_map/all_to_all | solution.py:51
  37.3 0.2 dynamic-update-slice
  37.5 29.9 %all-reduce = bf16[128]{0:T(256)(128)(2,1)S(1)} all-reduce(bf16[128]{0:T(256)(128)(2,1)S(1)} %dynamic-update-slice), channel_id=1, replica_groups=mesh['dp'=16,'expert'=2] {'dp'}, use_global_device_ids=true, to_apply=%add | all-reduce | flops 128 | bytes 512
  67.4 3.6 %fusion.3 = f32[128,448]{0,1:T(8,128)S(1)} fusion(bf16[128,4096]{1,0:T(8,128)(2,1)} %all-gather.5.cloned.1.call-done, bf16[1,448,4096]{2,1,0:T(8,128)(2,1)} %param.11), kind=kOutput, calls=%fused_computation.8 | convolution fusion | flops 469762048 | bytes 4947968 | tf_op jit(solution)/shard_map/dot_general | solution.py:16
  71.2 1.1 fusion.5
  72.3 25.7 %all-gather.3.cloned.1.call-done = bf16[128,4096]{1,0:T(8,128)(2,1)} async-done(((bf16[8,4096]{1,0:T(8,128)(2,1)}), bf16[128,4096]{1,0:T(8,128)(2,1)}) %all-gather.3.cloned.1.call-update) | async-done | bytes 1048592 | tf_op jit(solution)/shard_map/all_gather | solution.py:62
  98.1 3.5 %multiply_reduce_fusion = (f32[128]{0:T(128)S(1)}, bf16[128,448]{0,1:T(8,128)(2,1)S(1)}, f32[128,448]{0,1:T(8,128)S(1)}) fusion(f32[128,448]{0,1:T(8,128)S(1)} %fusion.5, f32[128,448]{0,1:T(8,128)S(1)} %fusion.3, bf16[128,4096]{1,0:T(8,128)(2,1)} %all-gather.3.cloned.1.call-done, bf16[1,448,4096]{2,1,0:T(8,128)(2,1)} %param.13), kind=kOutput, calls=%fused_computation.18 | convolution fusion | flops 470278016 | bytes 5521920 | tf_op jit(solution)/shard_map/dot_general | solution.py:16
  101.5 31.6 %all-reduce.1 = f32[128]{0:T(128)S(1)} all-reduce(f32[128]{0:T(128)S(1)} %get-tuple-element.6), channel_id=2, replica_groups=mesh['dp'=16,'expert'=2] {'dp'}, use_global_device_ids=true, to_apply=%region_6.7.clone | all-reduce | flops 128 | bytes 1024
  133.2 0.6 all_to_all.22
  133.9 3.2 %all-to-all-start.3 = ((f32[2,1,4]{2,1,0:T(1,128)}), f32[2,1,4]{2,1,0:T(1,128)S(1)}, u32[]{:S(2)}, u32[]{:S(2)}) async-start(f32[2,1,4]{2,1,0:T(1,128)} %bitcast.9), calls=%async_computation.3 | async-start | bytes 2048 | tf_op jit(solution)/shard_map/all_to_all | solution.py:79
  137.1 3.0 %fusion = bf16[1,448,4096]{2,1,0:T(8,128)(2,1)} fusion(bf16[128,4096]{1,0:T(8,128)(2,1)S(1)} %copy-done.1, f32[128,448]{0,1:T(8,128)S(1)} %fusion.3, f32[128,448]{0,1:T(8,128)S(1)} %fusion.5, f32[128,448]{0,1:T(8,128)S(1)} %get-tuple-element.12, f32[128]{0:T(128)S(1)} %convert_element_type.63), kind=kOutput, calls=%fused_computation.3 | convolution fusion | flops 472227840 | bytes 5407232 | tf_op jit(solution)/shard_map/dot_general | solution.py:10
  140.0 3.0 %fusion.1 = bf16[1,448,4096]{2,1,0:T(8,128)(2,1)} fusion(bf16[128,4096]{1,0:T(8,128)(2,1)S(1)} %copy-done.1, f32[128,448]{0,1:T(8,128)S(1)} %fusion.3, f32[128,448]{0,1:T(8,128)S(1)} %get-tuple-element.12, f32[128]{0:T(128)S(1)} %convert_element_type.63), kind=kOutput, calls=%fused_computation.4 | convolution fusion | flops 471998464 | bytes 5177856 | tf_op jit(solution)/shard_map/dot_general | solution.py:10
  143.0 3.0 %fusion.2 = bf16[1,448,4096]{2,1,0:T(8,128)(2,1)} fusion(bf16[128,448]{0,1:T(8,128)(2,1)S(1)} %get-tuple-element.7, bf16[128,4096]{1,0:T(8,128)(2,1)S(1)} %copy-done.2, f32[128]{0:T(128)S(1)} %convert_element_type.63), kind=kOutput, calls=%fused_computation.5 | convolution fusion | flops 473169920 | bytes 4833792 | tf_op jit(solution)/shard_map/dot_general | solution.py:10
  146.0 0.5 broadcast.75
  146.5 0.7 reduce.6
  147.3 0.7 fusion.16
  (36 shorter events, 1.6 us)
Async XLA Ops:
  7.2 3.6 %copy-start = (bf16[128,4096]{1,0:T(8,128)(2,1)S(1)}, bf16[128,4096]{1,0:T(8,128)(2,1)}, u32[]{:S(2)}) copy-start(bf16[128,4096]{1,0:T(8,128)(2,1)} %param.7) | copy-start | bytes 3145732
  7.2 26.3 %copy-start.4 = (u32[32]{0:T(128)S(1)}, u32[32]{0:T(128)}, u32[]{:S(2)}) copy-start(u32[32]{0:T(128)} %constant.20) | copy-start | bytes 388
  7.2 60.2 %all-gather.5.cloned.1.call-start = ((), (), s32[]{:S(2)}) async-start(), calls=%async_computation.5 | async-start | bytes 1114112 | tf_op jit(solution)/shard_map/all_gather | solution.py:61
  19.8 78.2 %all-gather.3.cloned.1.call-start = ((), (), s32[]{:S(2)}) async-start(), calls=%async_computation.4 | async-start | bytes 1114112 | tf_op jit(solution)/shard_map/all_gather | solution.py:62
  30.3 6.9 %all-to-all-start = ((bf16[2,1,4]{2,1,0:T(2,128)(2,1)}), bf16[2,1,4]{2,1,0:T(2,128)(2,1)S(1)}, u32[]{:S(2)}, u32[]{:S(2)}) async-start(bf16[2,1,4]{2,1,0:T(2,128)(2,1)} %all_to_all.24), calls=%async_computation | async-start | bytes 2048 | tf_op jit(solution)/shard_map/all_to_all | solution.py:51
  67.4 3.7 %copy-start.1 = (bf16[128,4096]{1,0:T(8,128)(2,1)S(1)}, bf16[128,4096]{1,0:T(8,128)(2,1)}, u32[]{:S(2)}) copy-start(bf16[128,4096]{1,0:T(8,128)(2,1)} %all-gather.5.cloned.1.call-done) | copy-start | bytes 3145732
  67.4 3.8 %copy-start.3 = (bf16[1,448,4096]{2,1,0:T(8,128)(2,1)S(1)}, bf16[1,448,4096]{2,1,0:T(8,128)(2,1)}, u32[]{:S(2)}) copy-start(bf16[1,448,4096]{2,1,0:T(8,128)(2,1)} %param.12) | copy-start | bytes 11010052
  133.9 12.2 %all-to-all-start.3 = ((f32[2,1,4]{2,1,0:T(1,128)}), f32[2,1,4]{2,1,0:T(1,128)S(1)}, u32[]{:S(2)}, u32[]{:S(2)}) async-start(f32[2,1,4]{2,1,0:T(1,128)} %bitcast.9), calls=%async_computation.3 | async-start | bytes 2048 | tf_op jit(solution)/shard_map/all_to_all | solution.py:79
  140.0 3.0 %copy-start.2 = (bf16[128,4096]{1,0:T(8,128)(2,1)S(1)}, bf16[128,4096]{1,0:T(8,128)(2,1)}, u32[]{:S(2)}) copy-start(bf16[128,4096]{1,0:T(8,128)(2,1)} %all-gather.3.cloned.1.call-done) | copy-start | bytes 3145732
Sparse Core Ops, SparseCore 0:
  20.0 38.3 all-gather.4
  61.1 36.8 all-gather.2
where the time goes:
time: 155 us
  blocking collectives  76.1 us (49%)
  waiting for transfers between devices  27.6 us (18%)
  matrix products  19.7 us (13%)
  between operations  15.5 us (10%)
  local copies, waits for them, and re-layouts  7.12 us (5%)
  starting transfers between devices  6.47 us (4%)
  other arithmetic  2.33 us (2%)
    unnamed x2, blocking collectives  61.5 us
    all_gather x1, waiting for transfers between devices, shards(): piece_dy = lax.all_gather(rows_dy, 'dp', axis=0, tiled=True)  25.7 us
    dot_general x3, matrix products, contract_rows(): lax.dot_general(left, right, (((0,), (0,)), ((), ())), preferred_element_...  8.95 us
    dot_general x3, matrix products, contract_cols(): lax.dot_general(left, right, (((1,), (1,)), ((), ())), preferred_element_...  8.24 us
    all_to_all x1, blocking collectives, shards(): lax.all_to_all(send_x.reshape(owners, ROW_CAPACITY, -1), 'expert', split_...  8.16 us
    all_to_all x1, blocking collectives, shards(): lax.all_to_all(send_dy.reshape(owners, ROW_CAPACITY, -1), 'expert', split...  6.5 us
    all_to_all x1, starting transfers between devices, shards(): lax.all_to_all(send_p.reshape(owners, ROW_CAPACITY), 'expert', split_axis...  3.19 us
    all_to_all x1, starting transfers between devices, shards(): lax.all_to_all(router_rows.reshape(owners, ROW_CAPACITY), 'expert', split...  3.19 us
  transfers between devices with their start and end apart: 4, of which 2 were waited for; matrix products, arithmetic and copies ran while one was open for 12% of the time, Pallas kernels for 0%

commit v1 on v0

v1 whole, which is shorter than its diff:
```python
import functools

import jax
import jax.numpy as jnp
from jax import lax
from jax.experimental import pallas as pl
from jax.experimental.pallas import tpu as pltpu
from jax.sharding import PartitionSpec as P

MESH = pl.DeviceIdType.MESH
F32 = jnp.float32
BF16 = jnp.bfloat16
BLOCK = 16
LINE = 4
CORES = 2


def iota(shape, dim):
    return lax.broadcasted_iota(jnp.int32, shape, dim)


def dot_nt(a, b):
    return lax.dot_general(a, b, (((1,), (1,)), ((), ())), preferred_element_type=F32)


def dot_tn(a, b):
    return lax.dot_general(a, b, (((0,), (0,)), ((), ())), preferred_element_type=F32)


def forward_kernel(
    n_dp, n_e, recv,
    ids_ref, prob_ref, tok_hbm, cot_hbm, gate_hbm, up_hbm, down_hbm,
    x_out, sdy_out, dg_out, du_out, hid_out, gp_out,
    tok, cot, wg, wu, wd, sbuf, ybuf, gbuf, rbuf, backbuf, vrow,
    load_sem, y_send, y_recv, up_send, dn_send, mid_send, core_send, g_recv,
    r_send, r_recv, b_send, b_recv,
):
    me = lax.axis_index("dp")
    ex = lax.axis_index("expert")
    n_t, width = tok.shape
    pieces = BLOCK // recv
    cols = width // pieces
    slots = n_e * BLOCK
    mid_n = n_dp // (LINE * CORES)
    core = me % CORES
    mid = (me // CORES) % mid_n
    line = me // (CORES * mid_n)

    loads = [
        pltpu.make_async_copy(src, dst, load_sem.at[k])
        for k, (src, dst) in enumerate(
            ((tok_hbm, tok), (cot_hbm, cot), (gate_hbm.at[0], wg), (up_hbm.at[0], wu),
             (down_hbm.at[0], wd))
        )
    ]
    for load in loads:
        load.start()

    barrier = pltpu.get_barrier_semaphore()
    for o in range(1, n_dp):
        pl.semaphore_signal(barrier, inc=1, device_id=((me + o) % n_dp, ex), device_id_type=MESH)
    for o in range(1, n_e):
        pl.semaphore_signal(barrier, inc=1, device_id=(me, (ex + o) % n_e), device_id_type=MESH)

    id0, id1 = ids_ref[:, 0:1], ids_ref[:, 1:2]
    p0, p1 = prob_ref[:, 0:1].astype(F32), prob_ref[:, 1:2].astype(F32)
    lane = iota((n_t, slots), 1)
    lane_e, lane_c, lane_s = lane // BLOCK, (lane % BLOCK) // recv, lane % recv
    first, second = id0 == lane_e, id1 == lane_e
    hits = jnp.where(first | second, 1.0, 0.0).astype(F32)
    earlier = jnp.where(iota((n_t, n_t), 1) < iota((n_t, n_t), 0), 1.0, 0.0).astype(BF16)
    rank = jnp.dot(earlier, hits.astype(BF16), preferred_element_type=F32)
    base = jnp.where(rank == lane_s.astype(F32), hits, 0.0)
    probs = (jnp.where(first, p0, 0.0) + jnp.where(second, p1, 0.0)) * base
    pick = [jnp.where(lane_c == c, base, 0.0).astype(BF16) for c in range(pieces)]
    send_p = dot_tn(probs.astype(BF16), jnp.ones((n_t, 128), BF16))
    loads[0].wait()
    loads[1].wait()
    send_x = sum(dot_tn(pick[c], tok[:, c * cols:(c + 1) * cols]) for c in range(pieces))
    send_dy = sum(dot_tn(pick[c], cot[:, c * cols:(c + 1) * cols]) for c in range(pieces))
    for e in range(n_e):
        rows = slice(e * BLOCK, (e + 1) * BLOCK)
        sbuf[e, :, 0:cols] = send_x[rows].astype(BF16)
        sbuf[e, :, cols:2 * cols] = send_dy[rows].astype(BF16)
        sbuf[e, :, 2 * cols:] = send_p[rows].astype(BF16)

    pl.semaphore_wait(barrier, n_dp - 1 + n_e - 1)

    y_copies = []
    for o in range(1, n_e):
        to = (ex + o) % n_e
        y_copies.append(pltpu.make_async_remote_copy(
            src_ref=sbuf.at[to], dst_ref=ybuf.at[ex],
            send_sem=y_send.at[to], recv_sem=y_recv.at[ex],
            device_id=(me, to), device_id_type=MESH))
    for copy in y_copies:
        copy.start()
    ybuf[ex] = sbuf[ex]
    for o in range(1, n_e):
        frm = (ex + o) % n_e
        pltpu.make_async_remote_copy(
            src_ref=sbuf.at[frm], dst_ref=ybuf.at[frm],
            send_sem=y_send.at[frm], recv_sem=y_recv.at[frm],
            device_id=(me, frm), device_id_type=MESH).wait_recv()

    rows_y = ybuf[...].reshape(slots, 2 * cols + 128)
    taken = jnp.where(rows_y[:, 2 * cols:2 * cols + 1].astype(F32) > 0.0, 1.0, 0.0)
    a, b = iota((slots, slots), 0), iota((slots, slots), 1)
    same = (a % BLOCK) // recv == (b % BLOCK) // recv
    ahead = (a // BLOCK < b // BLOCK) | ((a // BLOCK == b // BLOCK) & (a % recv < b % recv))
    place = jnp.sum(jnp.where(same & ahead, taken, 0.0), axis=0, keepdims=True)
    taken_row = jnp.sum(jnp.where(a == b, taken, 0.0), axis=0, keepdims=True)
    o_row, i_col = iota((BLOCK, slots), 0), iota((BLOCK, slots), 1)
    merge = jnp.where(
        ((i_col % BLOCK) // recv == o_row // recv) & (place == (o_row % recv).astype(F32)),
        taken_row, 0.0)
    gbuf[me] = jnp.dot(merge.astype(BF16), rows_y, preferred_element_type=F32).astype(BF16)

    def index(l, m, c):
        return (l * mid_n + m) * CORES + c

    def block_copy(src, sem, target):
        return pltpu.make_async_remote_copy(
            src_ref=gbuf.at[src], dst_ref=gbuf.at[src], send_sem=sem, recv_sem=g_recv.at[src],
            device_id=(target, ex), device_id_type=MESH)

    def up_copy(l):
        return block_copy(index(l, mid, core), up_send.at[l], index(line + 1, mid, core))

    def down_copy(l):
        return block_copy(index(l, mid, core), dn_send.at[l], index(line - 1, mid, core))

    def mid_copy(l, o):
        return block_copy(
            index(l, mid, core), mid_send.at[o, l], index(l * 0 + line, (mid + o) % mid_n, core))

    def core_copy(l, m):
        return block_copy(
            index(l, m, core), core_send.at[l, m], index(line, mid, (core + 1) % CORES))

    def spread(l):
        for o in range(1, mid_n):
            mid_copy(l, o).start()
        core_copy(l, mid).start()

    def arrived(src):
        block_copy(src, core_send.at[0, 0], me).wait_recv()

    def from_mid(l):
        for o in range(1, mid_n):
            m = (mid + o) % mid_n
            arrived(index(l, m, core))
            core_copy(l, m).start()

    pl.when(line + 1 < LINE)(lambda: up_copy(line).start())
    pl.when(line >= 1)(lambda: down_copy(line).start())
    spread(line)

    for d in range(1, LINE):
        @pl.when(line - d >= 0)
        def _():
            arrived(index(line - d, mid, core))
            pl.when(line + 1 < LINE)(lambda: up_copy(line - d).start())
            spread(line - d)

        @pl.when(line + d < LINE)
        def _():
            arrived(index(line + d, mid, core))
            pl.when(line >= 1)(lambda: down_copy(line + d).start())
            spread(line + d)

        if d == 1:
            from_mid(line)
        else:
            pl.when(line - (d - 1) >= 0)(lambda: from_mid(line - (d - 1)))
            pl.when(line + (d - 1) < LINE)(lambda: from_mid(line + (d - 1)))
    pl.when(line - (LINE - 1) >= 0)(lambda: from_mid(line - (LINE - 1)))
    pl.when(line + (LINE - 1) < LINE)(lambda: from_mid(line + (LINE - 1)))
    for l in range(LINE):
        for m in range(mid_n):
            arrived(index(l, m, (core + 1) % CORES))

    n_rows = n_dp * BLOCK
    rows = gbuf[...].reshape(n_rows, 2 * cols + 128)
    x, dy = rows[:, 0:cols], rows[:, cols:2 * cols]
    p_col = rows[:, 2 * cols:2 * cols + 1].astype(F32)
    x_out[...] = x
    sdy_out[...] = (p_col * dy.astype(F32)).astype(BF16)
    ra, rb = iota((n_rows, n_rows), 0), iota((n_rows, n_rows), 1)
    p_row = jnp.sum(jnp.where(ra == rb, p_col, 0.0), axis=0, keepdims=True)
    join = jnp.where((ra // BLOCK == rb // BLOCK) & (ra % recv == rb % recv), 1.0, 0.0).astype(BF16)
    hidden_n = wg.shape[0]
    piece_of = (iota((hidden_n, n_rows), 1) % BLOCK) // recv

    def project(w, v):
        if pieces == 1:
            return dot_nt(w[...], v)
        part = jnp.zeros((hidden_n, n_rows), F32)
        for c in range(pieces):
            part = jnp.where(piece_of == c, dot_nt(w[:, c * cols:(c + 1) * cols], v), part)
        high = part.astype(BF16)
        low = (part - high.astype(F32)).astype(BF16)
        return (jnp.dot(high, join, preferred_element_type=F32)
                + jnp.dot(low, join, preferred_element_type=F32))

    loads[2].wait()
    gate_pre = project(wg, x)
    loads[3].wait()
    up_pre = project(wu, x)
    loads[4].wait()
    pulled = project(wd, dy)
    sigma = 1.0 / (1.0 + jnp.exp(-gate_pre))
    silu = gate_pre * sigma
    hidden = (silu * up_pre).astype(BF16)
    rbuf[me] = jnp.sum(hidden.astype(F32) * pulled, axis=0, keepdims=True)

    r_copies = []
    for o in range(1, n_dp):
        to = (me + o) % n_dp
        r_copies.append(pltpu.make_async_remote_copy(
            src_ref=rbuf.at[me], dst_ref=rbuf.at[me],
            send_sem=r_send.at[to], recv_sem=r_recv.at[me],
            device_id=(to, ex), device_id_type=MESH))
    for copy in r_copies:
        copy.start()

    hid_out[...] = hidden
    d_hidden = p_row * pulled
    dg_out[...] = (d_hidden * up_pre * sigma * (1.0 + gate_pre * (1.0 - sigma))).astype(BF16)
    du_out[...] = (d_hidden * silu).astype(BF16)

    for o in range(1, n_dp):
        frm = (me + o) % n_dp
        pltpu.make_async_remote_copy(
            src_ref=rbuf.at[frm], dst_ref=rbuf.at[frm],
            send_sem=r_send.at[frm], recv_sem=r_recv.at[frm],
            device_id=(frm, ex), device_id_type=MESH).wait_recv()
    total = jnp.sum(rbuf[...], axis=0)
    mine = iota((BLOCK, n_rows), 1) == me * BLOCK + iota((BLOCK, n_rows), 0)
    router = jnp.sum(jnp.where(mine, total, 0.0), axis=1, keepdims=True)
    back = jnp.sum(merge * router, axis=0, keepdims=True)
    vrow[...] = jnp.zeros_like(vrow)
    vrow[:, 0:slots] = back

    b_copies = []
    for o in range(1, n_e):
        to = (ex + o) % n_e
        b_copies.append(pltpu.make_async_remote_copy(
            src_ref=vrow, dst_ref=backbuf.at[ex],
            send_sem=b_send.at[to], recv_sem=b_recv.at[ex],
            device_id=(me, to), device_id_type=MESH))
    for copy in b_copies:
        copy.start()
    backbuf[ex] = vrow[...]
    for o in range(1, n_e):
        frm = (ex + o) % n_e
        pltpu.make_async_remote_copy(
            src_ref=vrow, dst_ref=backbuf.at[frm],
            send_sem=b_send.at[frm], recv_sem=b_recv.at[frm],
            device_id=(me, frm), device_id_type=MESH).wait_recv()
    ka, kb = iota((128, slots), 0), iota((128, slots), 1)
    sums = jnp.zeros((8, slots), F32)
    for e in range(n_e):
        move = jnp.where((kb // BLOCK == e) & (ka == ex * BLOCK + kb % BLOCK), 1.0, 0.0).astype(F32)
        sums += jnp.dot(jnp.broadcast_to(backbuf[e], (8, 128)), move,
                        precision=lax.Precision.HIGHEST, preferred_element_type=F32)
    found = jnp.where(lane_c == 0, base, 0.0) * sums[0:1]
    gp_out[:, 0:1] = jnp.sum(jnp.where(first, found, 0.0), axis=1, keepdims=True)
    gp_out[:, 1:2] = jnp.sum(jnp.where(second, found, 0.0), axis=1, keepdims=True)

    for copy in y_copies + r_copies + b_copies:
        copy.wait_send()

    for l in range(LINE):
        @pl.when((line + 1 < LINE) & (l <= line))
        def _():
            up_copy(l).wait_send()

        @pl.when((line >= 1) & (l >= line))
        def _():
            down_copy(l).wait_send()

        for o in range(1, mid_n):
            mid_copy(l, o).wait_send()
        for m in range(mid_n):
            core_copy(l, m).wait_send()


def grads_kernel(recv, per_piece, x_ref, sdy_ref, dg_ref, du_ref, hid_ref, gg_ref, gu_ref, gd_ref):
    piece = pl.program_id(0) // per_piece
    keep = (iota(dg_ref.shape, 1) % BLOCK) // recv == piece

    def outer(d_ref, rows_ref, out_ref):
        d = jnp.where(keep, d_ref[...].astype(F32), 0.0).astype(BF16)
        out_ref[0] = jnp.dot(d, rows_ref[...], preferred_element_type=F32).astype(BF16)

    outer(dg_ref, x_ref, gg_ref)
    outer(du_ref, x_ref, gu_ref)
    outer(hid_ref, sdy_ref, gd_ref)


def shards(n_dp, n_e, tokens, cotangent, expert_ids, gate_probs, gate_w, up_w, down_w):
    n_t, width = tokens.shape
    hidden_n = gate_w.shape[1]
    recv = 2 * n_e
    pieces = BLOCK // recv
    cols = width // pieces
    wide = 2 * cols + 128
    n_rows = n_dp * BLOCK
    mid_n = n_dp // (LINE * CORES)
    any_spec = pl.BlockSpec(memory_space=pl.ANY)
    vmem = pl.BlockSpec(memory_space=pltpu.VMEM)
    dma = pltpu.SemaphoreType.DMA
    x, sdy, dg, du, hid, gp = pl.pallas_call(
        functools.partial(forward_kernel, n_dp, n_e, recv),
        out_shape=(
            jax.ShapeDtypeStruct((n_rows, cols), BF16),
            jax.ShapeDtypeStruct((n_rows, cols), BF16),
            jax.ShapeDtypeStruct((hidden_n, n_rows), BF16),
            jax.ShapeDtypeStruct((hidden_n, n_rows), BF16),
            jax.ShapeDtypeStruct((hidden_n, n_rows), BF16),
            jax.ShapeDtypeStruct((n_t, 2), F32),
        ),
        in_specs=[vmem, vmem] + [any_spec] * 5,
        out_specs=[vmem] * 6,
        scratch_shapes=[
            pltpu.VMEM((n_t, width), BF16),
            pltpu.VMEM((n_t, width), BF16),
            pltpu.VMEM((hidden_n, width), BF16),
            pltpu.VMEM((hidden_n, width), BF16),
            pltpu.VMEM((hidden_n, width), BF16),
            pltpu.VMEM((n_e, BLOCK, wide), BF16),
            pltpu.VMEM((n_e, BLOCK, wide), BF16),
            pltpu.VMEM((n_dp, BLOCK, wide), BF16),
            pltpu.VMEM((n_dp, 1, n_rows), F32),
            pltpu.VMEM((n_e, 1, 128), F32),
            pltpu.VMEM((1, 128), F32),
            dma((5,)),
            dma((n_e,)), dma((n_e,)),
            dma((LINE,)), dma((LINE,)), dma((mid_n, LINE)), dma((LINE, mid_n)), dma((n_dp,)),
            dma((n_dp,)), dma((n_dp,)), dma((n_e,)), dma((n_e,)),
        ],
        compiler_params=pltpu.CompilerParams(
            collective_id=0, has_side_effects=True, vmem_limit_bytes=48 * 1024 * 1024),
        name="route_and_forward",
    )(expert_ids, gate_probs, tokens, cotangent, gate_w, up_w, down_w)

    tile = 512
    per_piece = cols // tile
    whole = pl.BlockSpec((hidden_n, n_rows), lambda b: (0, 0))
    part = pl.BlockSpec((n_rows, tile), lambda b: (0, b % per_piece))
    grad = jax.ShapeDtypeStruct((1, hidden_n, width), BF16)
    out = pl.BlockSpec((1, hidden_n, tile), lambda b: (0, 0, b))
    gg, gu, gd = pl.pallas_call(
        functools.partial(grads_kernel, recv, per_piece),
        grid=(width // tile,),
        out_shape=(grad, grad, grad),
        in_specs=[part, part, whole, whole, whole],
        out_specs=[out, out, out],
        compiler_params=pltpu.CompilerParams(vmem_limit_bytes=32 * 1024 * 1024),
        name="outer_products",
    )(x, sdy, dg, du, hid)
    return gg, gu, gd, gp


def solution(mesh):
    in_specs = (
        P(("dp", "expert"), None),
        P(("dp", "expert"), None),
        P(("dp", "expert"), None),
        P(("dp", "expert"), None),
        P("expert", "dp", None),
        P("expert", "dp", None),
        P("expert", "dp", None),
    )
    out_specs = (
        P("expert", "dp", None),
        P("expert", "dp", None),
        P("expert", "dp", None),
        P(("dp", "expert"), None),
    )
    body = functools.partial(shards, mesh.shape["dp"], mesh.shape["expert"])
    return jax.shard_map(body, mesh=mesh, in_specs=in_specs, out_specs=out_specs, check_vma=False)
```

time: 155 us -> 48.1 us (0.31)
  blocking collectives: 76.1 us -> 0 us
  Pallas kernels: 0 us -> 42.6 us
  waiting for transfers between devices: 27.6 us -> 0 us
  matrix products: 19.7 us -> 0 us
  between operations: 15.5 us -> 0.65 us
  starting transfers between devices: 6.47 us -> 0 us
  local copies, waits for them, and re-layouts: 7.12 us -> 4.65 us
  other arithmetic: 2.33 us -> 0 us
    unnamed x2 -> x0, blocking collectives: 61.5 us -> none
    pallas_call x0 -> x2, Pallas kernels: none -> 42.6 us  [the longest x1 36 us: shards(): pl.pallas_call(functools.partial(forward_kernel, n_dp, n_e, recv), out_sh...]
    all_gather x2 -> x0, waiting for transfers between devices: 25.7 us -> none  [the longest x1 25.7 us: shards(): piece_dy = lax.all_gather(rows_dy, 'dp', axis=0, tiled=True)]
    dot_general x10 -> x0, matrix products: 19.7 us -> none  [the longest x3 8.95 us: contract_rows(): lax.dot_general(left, right, (((0,), (0,)), ((), ())), preferred_element_...]
    all_to_all x2 -> x0, blocking collectives: 14.7 us -> none  [the longest x1 8.16 us: shards(): lax.all_to_all(send_x.reshape(owners, ROW_CAPACITY, -1), 'expert', split_...]
    all_to_all x2 -> x0, starting transfers between devices: 6.39 us -> none  [the longest x1 3.19 us: shards(): lax.all_to_all(send_p.reshape(owners, ROW_CAPACITY), 'expert', split_axis...]
    unnamed x16 -> x7, local copies, waits for them, and re-layouts: 2.68 us -> 4.65 us
    all_to_all x3 -> x0, local copies, waits for them, and re-layouts: 1.81 us -> none  [the longest x2 1.16 us: shards(): lax.all_to_all(router_rows.reshape(owners, ROW_CAPACITY), 'expert', split...]
  transfers between devices with their start and end apart: 4 -> 0, of which waited for: 2 -> 0; matrix products, arithmetic and copies ran while one was open for 12% -> 0% of each run, Pallas kernels for 0% -> 0%
where the time goes in v1:
time: 48.1 us; the launch traced here: 47.9 us
  Pallas kernels  42.6 us (89%)
  local copies, waits for them, and re-layouts  4.65 us (10%)
  between operations  0.65 us (1%)
    pallas_call x1, Pallas kernels, shards(): pl.pallas_call(functools.partial(forward_kernel, n_dp, n_e, recv), out_sh...  36 us
    pallas_call x1, Pallas kernels, shards(): pl.pallas_call(functools.partial(grads_kernel, recv, per_piece), grid=(wi...  6.6 us
    unnamed x7, local copies, waits for them, and re-layouts  4.65 us

profile of v1, /device:TPU:0, one launch (start us, length us, event | category | flops | bytes accessed | tf_op | source)
XLA Modules:
  0.0 47.9 jit_solution(14314715212892169440)
XLA Ops:
  0.6 0.8 %copy.12.prob_ref = bf16[128,2]{1,0:T(8,128)(2,1)S(1)} copy(bf16[128,2]{0,1:T(2,128)(2,1)} %param.10) | data formatting | bytes 1024 | tf_op args[3]
  1.4 0.8 %copy.11.ids_ref = s32[128,2]{1,0:T(8,128)S(1)} copy(s32[128,2]{0,1:T(2,128)} %param.9) | data formatting | bytes 2048 | tf_op args[2]
  2.2 0.0 copy-start
  2.2 1.2 %copy-done = bf16[128,4096]{1,0:T(8,128)(2,1)S(1)} copy-done((bf16[128,4096]{1,0:T(8,128)(2,1)S(1)}, bf16[128,4096]{1,0:T(8,128)(2,1)}, u32[]{:S(2)}) %copy-start) | copy-done | bytes 1048600
  3.4 0.0 copy-start.1
  3.4 1.2 %copy-done.1 = bf16[128,4096]{1,0:T(8,128)(2,1)S(1)} copy-done((bf16[128,4096]{1,0:T(8,128)(2,1)S(1)}, bf16[128,4096]{1,0:T(8,128)(2,1)}, u32[]{:S(2)}) %copy-start.1) | copy-done | bytes 1048600
  4.7 36.0 %route_and_forward.1 = (bf16[256,1024]{1,0:T(8,128)(2,1)S(1)}, bf16[256,1024]{1,0:T(8,128)(2,1)S(1)}, bf16[448,256]{1,0:T(8,128)(2,1)S(1)}, bf16[448,256]{1,0:T(...) custom-call(s32[128,2]{1,0:T(8,128)S(1)} %copy.11.ids_ref, bf16[128,2]{1,0:T(8,128)(2,1)S(1)} %copy.12.prob_ref, ...), custom_call_target="tpu_custom_call" | custom-call | tf_op jit(solution)/shard_map/route_and_forward/pallas_call | solution.py:314
  40.6 0.6 %copy.13 = f32[128,2]{0,1:T(2,128)} copy(f32[128,2]{1,0:T(8,128)S(1)} %get-tuple-element.25) | data formatting | bytes 2048
  41.3 6.6 %outer_products.1 = (bf16[1,448,4096]{2,1,0:T(8,128)(2,1)}, bf16[1,448,4096]{2,1,0:T(8,128)(2,1)}, bf16[1,448,4096]{2,1,0:T(8,128)(2,1)}) custom-call(bf16[256,1024]{1,0:T(8,128)(2,1)S(1)} %get-tuple-element.13.x_ref, bf16[256,1024]{1,0:T(8,128)(2,1)S(1)} %get-tuple-element.14.sdy_ref, bf16[448,256]{1,0:T(8,128)(2,1)S(1)} %get-tuple-element.15.dg_ref, ...), custom_call_target="tpu_custom_call" | custom-call | tf_op jit(solution)/shard_map/outer_products/pallas_call | solution.py:354
Async XLA Ops:
  2.2 1.2 %copy-start = (bf16[128,4096]{1,0:T(8,128)(2,1)S(1)}, bf16[128,4096]{1,0:T(8,128)(2,1)}, u32[]{:S(2)}) copy-start(bf16[128,4096]{1,0:T(8,128)(2,1)} %tok_hbm.1) | copy-start | bytes 3145732
  3.4 1.2 %copy-start.1 = (bf16[128,4096]{1,0:T(8,128)(2,1)S(1)}, bf16[128,4096]{1,0:T(8,128)(2,1)}, u32[]{:S(2)}) copy-start(bf16[128,4096]{1,0:T(8,128)(2,1)} %cot_hbm.1) | copy-start | bytes 3145732

commit v2 on v1

v2 whole, which is shorter than its diff:
```python
import functools

import jax
import jax.numpy as jnp
from jax import lax
from jax.experimental import pallas as pl
from jax.experimental.pallas import tpu as pltpu
from jax.sharding import PartitionSpec as P

MESH = pl.DeviceIdType.MESH
F32 = jnp.float32
BF16 = jnp.bfloat16
BLOCK = 16
LINE = 4
CORES = 2


def iota(shape, dim):
    return lax.broadcasted_iota(jnp.int32, shape, dim)


def dot_nt(a, b):
    return lax.dot_general(a, b, (((1,), (1,)), ((), ())), preferred_element_type=F32)


def forward_kernel(
    n_dp, n_e, recv,
    ids_ref, prob_ref, tok_hbm, cot_hbm, gate_hbm, up_hbm, down_hbm,
    x_out, sdy_out, dg_out, du_out, hid_out, gp_out,
    tok, cot, wg, wu, wd, sx, sd, yx, yd, gx, gd, pre_g, pre_u, rbuf, backbuf, vrow,
    load_sem, y_send, y_recv, up_send, dn_send, mid_send, core_send, g_recv,
    r_send, r_recv, b_send, b_recv,
):
    me = lax.axis_index("dp")
    ex = lax.axis_index("expert")
    n_t, width = tok.shape
    pieces = BLOCK // recv
    cols = width // pieces
    slots = n_e * BLOCK
    mid_n = n_dp // (LINE * CORES)
    core = me % CORES
    mid = (me // CORES) % mid_n
    line = me // (CORES * mid_n)

    loads = [
        pltpu.make_async_copy(src, dst, load_sem.at[k])
        for k, (src, dst) in enumerate(
            ((tok_hbm, tok), (cot_hbm, cot), (gate_hbm.at[0], wg), (up_hbm.at[0], wu),
             (down_hbm.at[0], wd))
        )
    ]
    for load in loads:
        load.start()

    barrier = pltpu.get_barrier_semaphore()
    for o in range(1, n_dp):
        pl.semaphore_signal(barrier, inc=1, device_id=((me + o) % n_dp, ex), device_id_type=MESH)
    for o in range(1, n_e):
        pl.semaphore_signal(barrier, inc=1, device_id=(me, (ex + o) % n_e), device_id_type=MESH)

    id0, id1 = ids_ref[0:1, :], ids_ref[1:2, :]
    p0, p1 = prob_ref[0:1, :].astype(F32), prob_ref[1:2, :].astype(F32)
    row = iota((slots, n_t), 0)
    row_e, row_c, row_s = row // BLOCK, (row % BLOCK) // recv, row % recv
    first, second = id0 == row_e, id1 == row_e
    hits = jnp.where(first | second, 1.0, 0.0).astype(F32)
    earlier = jnp.where(iota((n_t, n_t), 0) < iota((n_t, n_t), 1), 1.0, 0.0).astype(BF16)
    rank = jnp.dot(hits.astype(BF16), earlier, preferred_element_type=F32)
    base = jnp.where(rank == row_s.astype(F32), hits, 0.0)
    probs = jnp.sum(
        (jnp.where(first, p0, 0.0) + jnp.where(second, p1, 0.0)) * base, axis=1, keepdims=True)
    pick = [jnp.where(row_c == c, base, 0.0).astype(BF16) for c in range(pieces)]

    def gather(src):
        return sum(
            jnp.dot(pick[c], src[:, c * cols:(c + 1) * cols], preferred_element_type=F32)
            for c in range(pieces)
        ).astype(BF16)

    vrow[...] = jnp.zeros_like(vrow)
    loads[0].wait()
    sx[:, :, 0:cols] = gather(tok).reshape(n_e, BLOCK, cols)
    sx[:, :, cols:] = jnp.broadcast_to(probs, (slots, 128)).astype(BF16).reshape(n_e, BLOCK, 128)
    pl.semaphore_wait(barrier, n_dp - 1 + n_e - 1)

    def y_copy(k, there, slot):
        src, dst = ((sx, yx), (sd, yd))[k]
        return pltpu.make_async_remote_copy(
            src_ref=src.at[there], dst_ref=dst.at[slot],
            send_sem=y_send.at[k, there], recv_sem=y_recv.at[k, slot],
            device_id=(me, there), device_id_type=MESH)

    others = [(ex + o) % n_e for o in range(1, n_e)]
    for e in others:
        y_copy(0, e, ex).start()
    yx[ex] = sx[ex]
    loads[1].wait()
    sd[...] = gather(cot).reshape(n_e, BLOCK, cols)
    for e in others:
        y_copy(1, e, ex).start()
    yd[ex] = sd[ex]

    def index(l, m, c):
        return (l * mid_n + m) * CORES + c

    def block_copy(k, src, sem, target):
        buf = (gx, gd)[k]
        return pltpu.make_async_remote_copy(
            src_ref=buf.at[src], dst_ref=buf.at[src], send_sem=sem, recv_sem=g_recv.at[k, src],
            device_id=(target, ex), device_id_type=MESH)

    def up_copy(k, l):
        return block_copy(k, index(l, mid, core), up_send.at[k, l], index(line + 1, mid, core))

    def down_copy(k, l):
        return block_copy(k, index(l, mid, core), dn_send.at[k, l], index(line - 1, mid, core))

    def mid_copy(k, l, o):
        return block_copy(
            k, index(l, mid, core), mid_send.at[k, o, l], index(line, (mid + o) % mid_n, core))

    def core_copy(k, l, m):
        return block_copy(
            k, index(l, m, core), core_send.at[k, l, m], index(line, mid, (core + 1) % CORES))

    def spread(k, l):
        for o in range(1, mid_n):
            mid_copy(k, l, o).start()
        core_copy(k, l, mid).start()

    def arrived(k, src):
        block_copy(k, src, core_send.at[k, 0, 0], me).wait_recv()

    def begin(k):
        pl.when(line + 1 < LINE)(lambda: up_copy(k, line).start())
        pl.when(line >= 1)(lambda: down_copy(k, line).start())
        spread(k, line)

    def along(k, d):
        @pl.when(line - d >= 0)
        def _():
            arrived(k, index(line - d, mid, core))
            pl.when(line + 1 < LINE)(lambda: up_copy(k, line - d).start())
            spread(k, line - d)

        @pl.when(line + d < LINE)
        def _():
            arrived(k, index(line + d, mid, core))
            pl.when(line >= 1)(lambda: down_copy(k, line + d).start())
            spread(k, line + d)

    def from_mid(k, l):
        for o in range(1, mid_n):
            m = (mid + o) % mid_n
            arrived(k, index(l, m, core))
            core_copy(k, l, m).start()

    def across(k, d):
        if d == 0:
            from_mid(k, line)
        else:
            pl.when(line - d >= 0)(lambda: from_mid(k, line - d))
            pl.when(line + d < LINE)(lambda: from_mid(k, line + d))

    def from_core(k):
        for l in range(LINE):
            for m in range(mid_n):
                arrived(k, index(l, m, (core + 1) % CORES))

    for e in others:
        y_copy(0, e, e).wait_recv()
    rows_y = yx[...].reshape(slots, cols + 128)
    taken = jnp.where(rows_y[:, cols:cols + 1].astype(F32) > 0.0, 1.0, 0.0)
    a, b = iota((slots, slots), 0), iota((slots, slots), 1)
    same = (a % BLOCK) // recv == (b % BLOCK) // recv
    ahead = (a // BLOCK < b // BLOCK) | ((a // BLOCK == b // BLOCK) & (a % recv < b % recv))
    place = jnp.sum(jnp.where(same & ahead, taken, 0.0), axis=0, keepdims=True)
    taken_row = jnp.sum(jnp.where(a == b, taken, 0.0), axis=0, keepdims=True)
    o_row, i_col = iota((BLOCK, slots), 0), iota((BLOCK, slots), 1)
    merge = jnp.where(
        ((i_col % BLOCK) // recv == o_row // recv) & (place == (o_row % recv).astype(F32)),
        taken_row, 0.0)
    gx[me] = jnp.dot(merge.astype(BF16), rows_y, preferred_element_type=F32).astype(BF16)
    begin(0)
    for e in others:
        y_copy(1, e, e).wait_recv()
    gd[me] = jnp.dot(
        merge.astype(BF16), yd[...].reshape(slots, cols), preferred_element_type=F32).astype(BF16)
    begin(1)
    for d in range(1, LINE):
        along(0, d)
        across(0, d - 1)
    along(1, 1)
    across(0, LINE - 1)
    from_core(0)

    n_rows = n_dp * BLOCK
    rows = gx[...].reshape(n_rows, cols + 128)
    x = rows[:, 0:cols]
    x_out[...] = x
    p_col = rows[:, cols:cols + 1].astype(F32)
    ra, rb = iota((n_rows, n_rows), 0), iota((n_rows, n_rows), 1)
    p_row = jnp.sum(jnp.where(ra == rb, p_col, 0.0), axis=0, keepdims=True)
    join = jnp.where((ra // BLOCK == rb // BLOCK) & (ra % recv == rb % recv), 1.0, 0.0).astype(BF16)
    hidden_n = wg.shape[0]
    piece_of = (iota((hidden_n, n_rows), 1) % BLOCK) // recv

    def some(w, v, part, wanted):
        for c in wanted:
            got = dot_nt(w[:, c * cols:(c + 1) * cols], v)
            part = got if part is None else jnp.where(piece_of == c, got, part)
        return part

    def joined(part):
        if pieces == 1:
            return part
        high = part.astype(BF16)
        low = (part - high.astype(F32)).astype(BF16)
        return (jnp.dot(high, join, preferred_element_type=F32)
                + jnp.dot(low, join, preferred_element_type=F32))

    early, late = range(0, (pieces + 1) // 2), range((pieces + 1) // 2, pieces)
    loads[2].wait()
    pre_g[...] = some(wg, x_out[...], None, early)
    along(1, 2)
    across(1, 0)
    pre_g[...] = joined(some(wg, x_out[...], pre_g[...], late))
    along(1, 3)
    across(1, 1)
    loads[3].wait()
    pre_u[...] = some(wu, x_out[...], None, early)
    across(1, 2)
    across(1, 3)
    pre_u[...] = joined(some(wu, x_out[...], pre_u[...], late))
    from_core(1)

    dy = gd[...].reshape(n_rows, cols)
    sdy_out[...] = (p_col * dy.astype(F32)).astype(BF16)
    loads[4].wait()
    pulled = joined(some(wd, dy, None, range(pieces)))
    gate_pre = pre_g[...]
    up_pre = pre_u[...]
    sigma = 1.0 / (1.0 + jnp.exp(-gate_pre))
    silu = gate_pre * sigma
    hidden = (silu * up_pre).astype(BF16)
    rbuf[me] = jnp.sum(hidden.astype(F32) * pulled, axis=0, keepdims=True)

    r_copies = []
    for o in range(1, n_dp):
        to = (me + o) % n_dp
        r_copies.append(pltpu.make_async_remote_copy(
            src_ref=rbuf.at[me], dst_ref=rbuf.at[me],
            send_sem=r_send.at[to], recv_sem=r_recv.at[me],
            device_id=(to, ex), device_id_type=MESH))
    for copy in r_copies:
        copy.start()

    hid_out[...] = hidden
    d_hidden = p_row * pulled
    dg_out[...] = (d_hidden * up_pre * sigma * (1.0 + gate_pre * (1.0 - sigma))).astype(BF16)
    du_out[...] = (d_hidden * silu).astype(BF16)

    for k in range(2):
        for e in others:
            y_copy(k, e, ex).wait_send()
        for l in range(LINE):
            @pl.when((line + 1 < LINE) & (l <= line))
            def _():
                up_copy(k, l).wait_send()

            @pl.when((line >= 1) & (l >= line))
            def _():
                down_copy(k, l).wait_send()

            for o in range(1, mid_n):
                mid_copy(k, l, o).wait_send()
            for m in range(mid_n):
                core_copy(k, l, m).wait_send()

    for o in range(1, n_dp):
        frm = (me + o) % n_dp
        pltpu.make_async_remote_copy(
            src_ref=rbuf.at[frm], dst_ref=rbuf.at[frm],
            send_sem=r_send.at[frm], recv_sem=r_recv.at[frm],
            device_id=(frm, ex), device_id_type=MESH).wait_recv()
    total = jnp.sum(rbuf[...], axis=0)
    mine = iota((BLOCK, n_rows), 1) == me * BLOCK + iota((BLOCK, n_rows), 0)
    router = jnp.sum(jnp.where(mine, total, 0.0), axis=1, keepdims=True)
    vrow[:, 0:slots] = jnp.sum(merge * router, axis=0, keepdims=True)

    b_copies = []
    for to in others:
        b_copies.append(pltpu.make_async_remote_copy(
            src_ref=vrow, dst_ref=backbuf.at[ex],
            send_sem=b_send.at[to], recv_sem=b_recv.at[ex],
            device_id=(me, to), device_id_type=MESH))
    for copy in b_copies:
        copy.start()
    backbuf[ex] = vrow[...]
    for copy in r_copies:
        copy.wait_send()
    for frm in others:
        pltpu.make_async_remote_copy(
            src_ref=vrow, dst_ref=backbuf.at[frm],
            send_sem=b_send.at[frm], recv_sem=b_recv.at[frm],
            device_id=(me, frm), device_id_type=MESH).wait_recv()
    va, vb = iota((BLOCK, slots), 0), iota((BLOCK, slots), 1)
    mine = vb == ex * BLOCK + va
    found = jnp.concatenate(
        [jnp.sum(jnp.where(mine, backbuf[e][:, 0:slots], 0.0), axis=1, keepdims=True)
         for e in range(n_e)], axis=0)
    found = jnp.where(row_c == 0, base, 0.0) * found
    gp_out[0:1, :] = jnp.sum(jnp.where(first, found, 0.0), axis=0, keepdims=True)
    gp_out[1:2, :] = jnp.sum(jnp.where(second, found, 0.0), axis=0, keepdims=True)
    for copy in b_copies:
        copy.wait_send()


def grads_kernel(recv, per_piece, x_ref, sdy_ref, dg_ref, du_ref, hid_ref, gg_ref, gu_ref, gd_ref):
    piece = pl.program_id(0) // per_piece
    keep = (iota(dg_ref.shape, 1) % BLOCK) // recv == piece

    def outer(d_ref, rows_ref, out_ref):
        d = jnp.where(keep, d_ref[...].astype(F32), 0.0).astype(BF16)
        out_ref[0] = jnp.dot(d, rows_ref[...], preferred_element_type=F32).astype(BF16)

    outer(dg_ref, x_ref, gg_ref)
    outer(du_ref, x_ref, gu_ref)
    outer(hid_ref, sdy_ref, gd_ref)


def shards(n_dp, n_e, tokens, cotangent, expert_ids, gate_probs, gate_w, up_w, down_w):
    n_t, width = tokens.shape
    hidden_n = gate_w.shape[1]
    recv = 2 * n_e
    pieces = BLOCK // recv
    cols = width // pieces
    wide = cols + 128
    n_rows = n_dp * BLOCK
    mid_n = n_dp // (LINE * CORES)
    any_spec = pl.BlockSpec(memory_space=pl.ANY)
    vmem = pl.BlockSpec(memory_space=pltpu.VMEM)
    dma = pltpu.SemaphoreType.DMA
    x, sdy, dg, du, hid, gp = pl.pallas_call(
        functools.partial(forward_kernel, n_dp, n_e, recv),
        out_shape=(
            jax.ShapeDtypeStruct((n_rows, cols), BF16),
            jax.ShapeDtypeStruct((n_rows, cols), BF16),
            jax.ShapeDtypeStruct((hidden_n, n_rows), BF16),
            jax.ShapeDtypeStruct((hidden_n, n_rows), BF16),
            jax.ShapeDtypeStruct((hidden_n, n_rows), BF16),
            jax.ShapeDtypeStruct((2, n_t), F32),
        ),
        in_specs=[vmem, vmem] + [any_spec] * 5,
        out_specs=[vmem] * 6,
        scratch_shapes=[
            pltpu.VMEM((n_t, width), BF16),
            pltpu.VMEM((n_t, width), BF16),
            pltpu.VMEM((hidden_n, width), BF16),
            pltpu.VMEM((hidden_n, width), BF16),
            pltpu.VMEM((hidden_n, width), BF16),
            pltpu.VMEM((n_e, BLOCK, wide), BF16),
            pltpu.VMEM((n_e, BLOCK, cols), BF16),
            pltpu.VMEM((n_e, BLOCK, wide), BF16),
            pltpu.VMEM((n_e, BLOCK, cols), BF16),
            pltpu.VMEM((n_dp, BLOCK, wide), BF16),
            pltpu.VMEM((n_dp, BLOCK, cols), BF16),
            pltpu.VMEM((hidden_n, n_rows), F32),
            pltpu.VMEM((hidden_n, n_rows), F32),
            pltpu.VMEM((n_dp, 1, n_rows), F32),
            pltpu.VMEM((n_e, 1, 128), F32),
            pltpu.VMEM((1, 128), F32),
            dma((5,)),
            dma((2, n_e)), dma((2, n_e)),
            dma((2, LINE)), dma((2, LINE)), dma((2, mid_n, LINE)), dma((2, LINE, mid_n)),
            dma((2, n_dp)),
            dma((n_dp,)), dma((n_dp,)), dma((n_e,)), dma((n_e,)),
        ],
        compiler_params=pltpu.CompilerParams(
            collective_id=0, has_side_effects=True, vmem_limit_bytes=60 * 1024 * 1024),
        name="route_and_forward",
    )(expert_ids.T, gate_probs.T, tokens, cotangent, gate_w, up_w, down_w)

    tile = 512
    per_piece = cols // tile
    whole = pl.BlockSpec((hidden_n, n_rows), lambda b: (0, 0))
    part = pl.BlockSpec((n_rows, tile), lambda b: (0, b % per_piece))
    grad = jax.ShapeDtypeStruct((1, hidden_n, width), BF16)
    out = pl.BlockSpec((1, hidden_n, tile), lambda b: (0, 0, b))
    gg, gu, gd = pl.pallas_call(
        functools.partial(grads_kernel, recv, per_piece),
        grid=(width // tile,),
        out_shape=(grad, grad, grad),
        in_specs=[part, part, whole, whole, whole],
        out_specs=[out, out, out],
        compiler_params=pltpu.CompilerParams(vmem_limit_bytes=60 * 1024 * 1024),
        name="outer_products",
    )(x, sdy, dg, du, hid)
    return gg, gu, gd, gp.T


def solution(mesh):
    in_specs = (
        P(("dp", "expert"), None),
        P(("dp", "expert"), None),
        P(("dp", "expert"), None),
        P(("dp", "expert"), None),
        P("expert", "dp", None),
        P("expert", "dp", None),
        P("expert", "dp", None),
    )
    out_specs = (
        P("expert", "dp", None),
        P("expert", "dp", None),
        P("expert", "dp", None),
        P(("dp", "expert"), None),
    )
    body = functools.partial(shards, mesh.shape["dp"], mesh.shape["expert"])
    return jax.shard_map(body, mesh=mesh, in_specs=in_specs, out_specs=out_specs, check_vma=False)
```

time: 48.1 us -> 50 us (1.040)
  Pallas kernels: 42.6 us -> 47.9 us
  local copies, waits for them, and re-layouts: 4.65 us -> 1.23 us
    unnamed x7 -> x1, local copies, waits for them, and re-layouts: 4.65 us -> 1.23 us
    pallas_call x1, Pallas kernels: 36 us -> 38.7 us  [shards(): pl.pallas_call(functools.partial(forward_kernel, n_dp, n_e, recv), out_sh...]
    pallas_call x1, Pallas kernels: 6.6 us -> 9.14 us  [shards(): pl.pallas_call(functools.partial(grads_kernel, recv, per_piece), grid=(wi...]
where the time goes in v2:
time: 50 us; the launch traced here: 49.7 us
  Pallas kernels  47.9 us (96%)
  local copies, waits for them, and re-layouts  1.23 us (2%)
  between operations  0.64 us (1%)
    pallas_call x1, Pallas kernels, shards(): pl.pallas_call(functools.partial(forward_kernel, n_dp, n_e, recv), out_sh...  38.7 us
    pallas_call x1, Pallas kernels, shards(): pl.pallas_call(functools.partial(grads_kernel, recv, per_piece), grid=(wi...  9.14 us
    unnamed x1, local copies, waits for them, and re-layouts  1.23 us

profile of v2, /device:TPU:0, one launch (start us, length us, event | category | flops | bytes accessed | tf_op | source)
XLA Modules:
  0.0 49.7 jit_solution(2311815119969721242)
XLA Ops:
  0.6 38.7 %route_and_forward.1 = (bf16[256,1024]{1,0:T(8,128)(2,1)}, bf16[256,1024]{1,0:T(8,128)(2,1)}, bf16[448,256]{1,0:T(8,128)(2,1)}, bf16[448,256]{1,0:T(8,128)(2,1)}...) custom-call(s32[2,128]{1,0:T(2,128)} %bitcast.4, bf16[2,128]{1,0:T(2,128)(2,1)} %bitcast.5, bf16[128,4096]{1,0:T(8,128)(2,1)} %tok_hbm.1, ...), custom_call_target="tpu_custom_call" | custom-call | tf_op jit(solution)/shard_map/route_and_forward/pallas_call | solution.py:344
  39.4 9.1 %outer_products.1 = (bf16[1,448,4096]{2,1,0:T(8,128)(2,1)}, bf16[1,448,4096]{2,1,0:T(8,128)(2,1)}, bf16[1,448,4096]{2,1,0:T(8,128)(2,1)}) custom-call(bf16[256,1024]{1,0:T(8,128)(2,1)} %get-tuple-element.13.x_ref, bf16[256,1024]{1,0:T(8,128)(2,1)} %get-tuple-element.14.sdy_ref, bf16[448,256]{1,0:T(8,128)(2,1)} %get-tuple-element.15.dg_ref, ...), custom_call_target="tpu_custom_call" | custom-call | tf_op jit(solution)/shard_map/outer_products/pallas_call | solution.py:390
  48.5 1.2 %copy.12 = f32[128,2]{0,1:T(2,128)} copy(f32[128,2]{0,1:T(2,128)} %bitcast.3) | data formatting | bytes 2048

commit v3 on v2

--- a/solution.py
+++ b/solution.py
@@ -27,9 +27,8 @@
     n_dp, n_e, recv,
     ids_ref, prob_ref, tok_hbm, cot_hbm, gate_hbm, up_hbm, down_hbm,
     x_out, sdy_out, dg_out, du_out, hid_out, gp_out,
-    tok, cot, wg, wu, wd, sx, sd, yx, yd, gx, gd, pre_g, pre_u, rbuf, backbuf, vrow,
-    load_sem, y_send, y_recv, up_send, dn_send, mid_send, core_send, g_recv,
-    r_send, r_recv, b_send, b_recv,
+    tok, cot, wg, wu, wd, sx, sd, yx, yd, gx, gd, pre_g, pre_u, rbuf,
+    load_sem, y_send, y_recv, z_send, mid_send, core_send, g_recv, r_send, r_recv,
 ):
     me = lax.axis_index("dp")
     ex = lax.axis_index("expert")
@@ -53,10 +52,15 @@
         load.start()
 
     barrier = pltpu.get_barrier_semaphore()
-    for o in range(1, n_dp):
-        pl.semaphore_signal(barrier, inc=1, device_id=((me + o) % n_dp, ex), device_id_type=MESH)
-    for o in range(1, n_e):
-        pl.semaphore_signal(barrier, inc=1, device_id=(me, (ex + o) % n_e), device_id_type=MESH)
+    n_all = n_dp * n_e
+    flat = me * n_e + ex
+
+    def greet(o, carry):
+        to = (flat + o) % n_all
+        pl.semaphore_signal(barrier, inc=1, device_id=(to // n_e, to % n_e), device_id_type=MESH)
+        return carry
+
+    lax.fori_loop(1, n_all, greet, 0)
 
     id0, id1 = ids_ref[0:1, :], ids_ref[1:2, :]
     p0, p1 = prob_ref[0:1, :].astype(F32), prob_ref[1:2, :].astype(F32)
@@ -77,11 +81,15 @@
             for c in range(pieces)
         ).astype(BF16)
 
-    vrow[...] = jnp.zeros_like(vrow)
     loads[0].wait()
     sx[:, :, 0:cols] = gather(tok).reshape(n_e, BLOCK, cols)
-    sx[:, :, cols:] = jnp.broadcast_to(probs, (slots, 128)).astype(BF16).reshape(n_e, BLOCK, 128)
-    pl.semaphore_wait(barrier, n_dp - 1 + n_e - 1)
+    counts = jnp.sum(hits, axis=1, keepdims=True)
+    tail = jnp.broadcast_to(probs, (slots, 128))
+    spot = iota((slots, 128), 1)
+    for e in range(n_e):
+        tail = jnp.where(spot == 64 + e, counts[e * BLOCK:e * BLOCK + 1, :], tail)
+    sx[:, :, cols:] = tail.astype(BF16).reshape(n_e, BLOCK, 128)
+    pl.semaphore_wait(barrier, n_all - 1)
 
     def y_copy(k, there, slot):
         src, dst = ((sx, yx), (sd, yd))[k]
@@ -100,6 +108,8 @@
         y_copy(1, e, ex).start()
     yd[ex] = sd[ex]
 
+    line_of = (line, line + 1 - 2 * (line % 2), (line + 2) % LINE, LINE - 1 - line)
+
     def index(l, m, c):
         return (l * mid_n + m) * CORES + c
 
@@ -109,11 +119,8 @@
             src_ref=buf.at[src], dst_ref=buf.at[src], send_sem=sem, recv_sem=g_recv.at[k, src],
             device_id=(target, ex), device_id_type=MESH)
 
-    def up_copy(k, l):
-        return block_copy(k, index(l, mid, core), up_send.at[k, l], index(line + 1, mid, core))
-
-    def down_copy(k, l):
-        return block_copy(k, index(l, mid, core), dn_send.at[k, l], index(line - 1, mid, core))
+    def line_copy(k, q):
+        return block_copy(k, me, z_send.at[k, q], index(line_of[q], mid, core))
 
     def mid_copy(k, l, o):
         return block_copy(
@@ -132,35 +139,19 @@
         block_copy(k, src, core_send.at[k, 0, 0], me).wait_recv()
 
     def begin(k):
-        pl.when(line + 1 < LINE)(lambda: up_copy(k, line).start())
-        pl.when(line >= 1)(lambda: down_copy(k, line).start())
+        for q in range(1, LINE):
+            line_copy(k, q).start()
         spread(k, line)
 
-    def along(k, d):
-        @pl.when(line - d >= 0)
-        def _():
-            arrived(k, index(line - d, mid, core))
-            pl.when(line + 1 < LINE)(lambda: up_copy(k, line - d).start())
-            spread(k, line - d)
-
-        @pl.when(line + d < LINE)
-        def _():
-            arrived(k, index(line + d, mid, core))
-            pl.when(line >= 1)(lambda: down_copy(k, line + d).start())
-            spread(k, line + d)
-
-    def from_mid(k, l):
+    def along(k, q):
+        arrived(k, index(line_of[q], mid, core))
+        spread(k, line_of[q])
+
+    def across(k, q):
         for o in range(1, mid_n):
             m = (mid + o) % mid_n
-            arrived(k, index(l, m, core))
-            core_copy(k, l, m).start()
-
-    def across(k, d):
-        if d == 0:
-            from_mid(k, line)
-        else:
-            pl.when(line - d >= 0)(lambda: from_mid(k, line - d))
-            pl.when(line + d < LINE)(lambda: from_mid(k, line + d))
+            arrived(k, index(line_of[q], m, core))
+            core_copy(k, line_of[q], m).start()
 
     def from_core(k):
         for l in range(LINE):
@@ -187,11 +178,12 @@
     gd[me] = jnp.dot(
         merge.astype(BF16), yd[...].reshape(slots, cols), preferred_element_type=F32).astype(BF16)
     begin(1)
-    for d in range(1, LINE):
-        along(0, d)
-        across(0, d - 1)
+    for q in range(1, LINE):
+        along(0, q)
+        across(0, q - 1)
+    across(0, LINE - 1)
     along(1, 1)
-    across(0, LINE - 1)
+    along(1, 2)
     from_core(0)
 
     n_rows = n_dp * BLOCK
@@ -221,17 +213,16 @@
 
     early, late = range(0, (pieces + 1) // 2), range((pieces + 1) // 2, pieces)
     loads[2].wait()
-    pre_g[...] = some(wg, x_out[...], None, early)
-    along(1, 2)
+    pre_g[...] = some(wg, x, None, early)
+    along(1, 3)
     across(1, 0)
     pre_g[...] = joined(some(wg, x_out[...], pre_g[...], late))
-    along(1, 3)
     across(1, 1)
     loads[3].wait()
     pre_u[...] = some(wu, x_out[...], None, early)
     across(1, 2)
+    pre_u[...] = joined(some(wu, x_out[...], pre_u[...], late))
     across(1, 3)
-    pre_u[...] = joined(some(wu, x_out[...], pre_u[...], late))
     from_core(1)
 
     dy = gd[...].reshape(n_rows, cols)
@@ -243,17 +234,21 @@
     sigma = 1.0 / (1.0 + jnp.exp(-gate_pre))
     silu = gate_pre * sigma
     hidden = (silu * up_pre).astype(BF16)
-    rbuf[me] = jnp.sum(hidden.astype(F32) * pulled, axis=0, keepdims=True)
-
-    r_copies = []
-    for o in range(1, n_dp):
-        to = (me + o) % n_dp
-        r_copies.append(pltpu.make_async_remote_copy(
-            src_ref=rbuf.at[me], dst_ref=rbuf.at[me],
-            send_sem=r_send.at[to], recv_sem=r_recv.at[me],
-            device_id=(to, ex), device_id_type=MESH))
-    for copy in r_copies:
-        copy.start()
+    rbuf[ex, me] = jnp.sum(hidden.astype(F32) * pulled, axis=0, keepdims=True)
+
+    def router_copy(o, slot):
+        to = (flat + o) % n_all
+        there = ex if slot else to % n_e, me if slot else to // n_e
+        return pltpu.make_async_remote_copy(
+            src_ref=rbuf.at[there], dst_ref=rbuf.at[there],
+            send_sem=r_send.at[o], recv_sem=r_recv.at[there],
+            device_id=(to // n_e, to % n_e), device_id_type=MESH)
+
+    def send_router(o, carry):
+        router_copy(o, True).start()
+        return carry
+
+    lax.fori_loop(1, n_all, send_router, 0)
 
     hid_out[...] = hidden
     d_hidden = p_row * pulled
@@ -263,60 +258,43 @@
     for k in range(2):
         for e in others:
             y_copy(k, e, ex).wait_send()
+        for q in range(1, LINE):
+            line_copy(k, q).wait_send()
         for l in range(LINE):
-            @pl.when((line + 1 < LINE) & (l <= line))
-            def _():
-                up_copy(k, l).wait_send()
-
-            @pl.when((line >= 1) & (l >= line))
-            def _():
-                down_copy(k, l).wait_send()
-
             for o in range(1, mid_n):
                 mid_copy(k, l, o).wait_send()
             for m in range(mid_n):
                 core_copy(k, l, m).wait_send()
 
-    for o in range(1, n_dp):
-        frm = (me + o) % n_dp
-        pltpu.make_async_remote_copy(
-            src_ref=rbuf.at[frm], dst_ref=rbuf.at[frm],
-            send_sem=r_send.at[frm], recv_sem=r_recv.at[frm],
-            device_id=(frm, ex), device_id_type=MESH).wait_recv()
-    total = jnp.sum(rbuf[...], axis=0)
-    mine = iota((BLOCK, n_rows), 1) == me * BLOCK + iota((BLOCK, n_rows), 0)
-    router = jnp.sum(jnp.where(mine, total, 0.0), axis=1, keepdims=True)
-    vrow[:, 0:slots] = jnp.sum(merge * router, axis=0, keepdims=True)
-
-    b_copies = []
-    for to in others:
-        b_copies.append(pltpu.make_async_remote_copy(
-            src_ref=vrow, dst_ref=backbuf.at[ex],
-            send_sem=b_send.at[to], recv_sem=b_recv.at[ex],
-            device_id=(me, to), device_id_type=MESH))
-    for copy in b_copies:
-        copy.start()
-    backbuf[ex] = vrow[...]
-    for copy in r_copies:
-        copy.wait_send()
-    for frm in others:
-        pltpu.make_async_remote_copy(
-            src_ref=vrow, dst_ref=backbuf.at[frm],
-            send_sem=b_send.at[frm], recv_sem=b_recv.at[frm],
-            device_id=(me, frm), device_id_type=MESH).wait_recv()
-    va, vb = iota((BLOCK, slots), 0), iota((BLOCK, slots), 1)
-    mine = vb == ex * BLOCK + va
-    found = jnp.concatenate(
-        [jnp.sum(jnp.where(mine, backbuf[e][:, 0:slots], 0.0), axis=1, keepdims=True)
-         for e in range(n_e)], axis=0)
-    found = jnp.where(row_c == 0, base, 0.0) * found
+    def get_router(o, carry):
+        router_copy(o, False).wait_recv()
+        return carry
+
+    lax.fori_loop(1, n_all, get_router, 0)
+
+    before = jnp.zeros((1, 128), F32)
+    for e in range(n_e):
+        before += jnp.where(e < ex, yx[e, 0:1, cols:].astype(F32), 0.0)
+    found = []
+    r_row, r_lane = iota((BLOCK, n_rows), 0), iota((BLOCK, n_rows), 1)
+    for e in range(n_e):
+        total = jnp.sum(rbuf[e], axis=0)
+        place = (me * BLOCK + r_row % recv).astype(F32) + before[:, 64 + e:65 + e]
+        found.append(jnp.sum(
+            jnp.where(r_lane.astype(F32) == place, total, 0.0), axis=1, keepdims=True))
+    found = jnp.where(row_c == 0, base, 0.0) * jnp.concatenate(found, axis=0)
     gp_out[0:1, :] = jnp.sum(jnp.where(first, found, 0.0), axis=0, keepdims=True)
     gp_out[1:2, :] = jnp.sum(jnp.where(second, found, 0.0), axis=0, keepdims=True)
-    for copy in b_copies:
-        copy.wait_send()
-
-
-def grads_kernel(recv, per_piece, x_ref, sdy_ref, dg_ref, du_ref, hid_ref, gg_ref, gu_ref, gd_ref):
+
+    def sent_router(o, carry):
+        router_copy(o, True).wait_send()
+        return carry
+
+    lax.fori_loop(1, n_all, sent_router, 0)
+
+
+def grads_kernel(recv, per_piece, x_ref, sdy_ref, dg_ref, du_ref, hid_ref, gp_ref,
+                 gg_ref, gu_ref, gd_ref, gp_out):
     piece = pl.program_id(0) // per_piece
     keep = (iota(dg_ref.shape, 1) % BLOCK) // recv == piece
 
@@ -327,6 +305,7 @@
     outer(dg_ref, x_ref, gg_ref)
     outer(du_ref, x_ref, gu_ref)
     outer(hid_ref, sdy_ref, gd_ref)
+    gp_out[...] = gp_ref[...]
 
 
 def shards(n_dp, n_e, tokens, cotangent, expert_ids, gate_probs, gate_w, up_w, down_w):
@@ -338,7 +317,7 @@
     wide = cols + 128
     n_rows = n_dp * BLOCK
     mid_n = n_dp // (LINE * CORES)
-    any_spec = pl.BlockSpec(memory_space=pl.ANY)
+    hbm = pl.BlockSpec(memory_space=pltpu.HBM)
     vmem = pl.BlockSpec(memory_space=pltpu.VMEM)
     dma = pltpu.SemaphoreType.DMA
     x, sdy, dg, du, hid, gp = pl.pallas_call(
@@ -351,7 +330,7 @@
             jax.ShapeDtypeStruct((hidden_n, n_rows), BF16),
             jax.ShapeDtypeStruct((2, n_t), F32),
         ),
-        in_specs=[vmem, vmem] + [any_spec] * 5,
+        in_specs=[vmem, vmem] + [hbm] * 5,
         out_specs=[vmem] * 6,
         scratch_shapes=[
             pltpu.VMEM((n_t, width), BF16),
@@ -367,17 +346,14 @@
             pltpu.VMEM((n_dp, BLOCK, cols), BF16),
             pltpu.VMEM((hidden_n, n_rows), F32),
             pltpu.VMEM((hidden_n, n_rows), F32),
-            pltpu.VMEM((n_dp, 1, n_rows), F32),
-            pltpu.VMEM((n_e, 1, 128), F32),
-            pltpu.VMEM((1, 128), F32),
+            pltpu.VMEM((n_e, n_dp, 1, n_rows), F32),
             dma((5,)),
             dma((2, n_e)), dma((2, n_e)),
-            dma((2, LINE)), dma((2, LINE)), dma((2, mid_n, LINE)), dma((2, LINE, mid_n)),
-            dma((2, n_dp)),
-            dma((n_dp,)), dma((n_dp,)), dma((n_e,)), dma((n_e,)),
+            dma((2, LINE)), dma((2, mid_n, LINE)), dma((2, LINE, mid_n)), dma((2, n_dp)),
+            dma((n_dp * n_e,)), dma((n_e, n_dp)),
         ],
         compiler_params=pltpu.CompilerParams(
-            collective_id=0, has_side_effects=True, vmem_limit_bytes=60 * 1024 * 1024),
+            collective_id=0, has_side_effects=True, vmem_limit_bytes=48 * 1024 * 1024),
         name="route_and_forward",
     )(expert_ids.T, gate_probs.T, tokens, cotangent, gate_w, up_w, down_w)
 
@@ -387,15 +363,16 @@
     part = pl.BlockSpec((n_rows, tile), lambda b: (0, b % per_piece))
     grad = jax.ShapeDtypeStruct((1, hidden_n, width), BF16)
     out = pl.BlockSpec((1, hidden_n, tile), lambda b: (0, 0, b))
-    gg, gu, gd = pl.pallas_call(
+    small = pl.BlockSpec((2, n_t), lambda b: (0, 0))
+    gg, gu, gd, gp = pl.pallas_call(
         functools.partial(grads_kernel, recv, per_piece),
         grid=(width // tile,),
-        out_shape=(grad, grad, grad),
-        in_specs=[part, part, whole, whole, whole],
-        out_specs=[out, out, out],
-        compiler_params=pltpu.CompilerParams(vmem_limit_bytes=60 * 1024 * 1024),
+        out_shape=(grad, grad, grad, jax.ShapeDtypeStruct((2, n_t), F32)),
+        in_specs=[part, part, whole, whole, whole, small],
+        out_specs=[out, out, out, small],
+        compiler_params=pltpu.CompilerParams(vmem_limit_bytes=32 * 1024 * 1024),
         name="outer_products",
-    )(x, sdy, dg, du, hid)
+    )(x, sdy, dg, du, hid, gp)
     return gg, gu, gd, gp.T
 
 

time: 50 us -> 44 us (0.88)
  Pallas kernels: 47.9 us -> 39.4 us
  local copies, waits for them, and re-layouts: 1.23 us -> 3.78 us
    pallas_call x1, Pallas kernels: 38.7 us -> 32.7 us  [shards(): pl.pallas_call(functools.partial(forward_kernel, n_dp, n_e, recv), out_sh...]
    unnamed x1 -> x8, local copies, waits for them, and re-layouts: 1.23 us -> 3.78 us
    pallas_call x1, Pallas kernels: 9.14 us -> 6.66 us  [shards(): pl.pallas_call(functools.partial(grads_kernel, recv, per_piece), grid=(wi...]
where the time goes in v3:
time: 44 us; the launch traced here: 43.8 us
  Pallas kernels  39.4 us (90%)
  local copies, waits for them, and re-layouts  3.78 us (9%)
  between operations  0.65 us (1%)
    pallas_call x1, Pallas kernels, shards(): pl.pallas_call(functools.partial(forward_kernel, n_dp, n_e, recv), out_sh...  32.7 us
    pallas_call x1, Pallas kernels, shards(): pl.pallas_call(functools.partial(grads_kernel, recv, per_piece), grid=(wi...  6.66 us
    unnamed x8, local copies, waits for them, and re-layouts  3.78 us

profile of v3, /device:TPU:0, one launch (start us, length us, event | category | flops | bytes accessed | tf_op | source)
XLA Modules:
  0.0 43.8 jit_solution(15941580902404920212)
XLA Ops:
  0.6 0.0 copy-start
  0.6 1.2 %copy-done = bf16[128,4096]{1,0:T(8,128)(2,1)S(1)} copy-done((bf16[128,4096]{1,0:T(8,128)(2,1)S(1)}, bf16[128,4096]{1,0:T(8,128)(2,1)}, u32[]{:S(2)}) %copy-start) | copy-done | bytes 1048600
  1.9 0.0 copy-start.1
  1.9 1.2 %copy-done.1 = bf16[128,4096]{1,0:T(8,128)(2,1)S(1)} copy-done((bf16[128,4096]{1,0:T(8,128)(2,1)S(1)}, bf16[128,4096]{1,0:T(8,128)(2,1)}, u32[]{:S(2)}) %copy-start.1) | copy-done | bytes 1048600
  3.1 0.0 copy-start.2
  3.1 0.7 %copy-done.2 = s32[128,2]{0,1:T(2,128)S(1)} copy-done((s32[128,2]{0,1:T(2,128)S(1)}, s32[128,2]{0,1:T(2,128)}, u32[]{:S(2)}) %copy-start.2) | copy-done | bytes 1048
  3.8 0.0 copy-start.3
  3.8 0.7 %copy-done.3 = bf16[128,2]{0,1:T(2,128)(2,1)S(1)} copy-done((bf16[128,2]{0,1:T(2,128)(2,1)S(1)}, bf16[128,2]{0,1:T(2,128)(2,1)}, u32[]{:S(2)}) %copy-start.3) | copy-done | bytes 536
  4.4 32.7 %route_and_forward.1 = (bf16[256,1024]{1,0:T(8,128)(2,1)S(1)}, bf16[256,1024]{1,0:T(8,128)(2,1)S(1)}, bf16[448,256]{1,0:T(8,128)(2,1)S(1)}, bf16[448,256]{1,0:T(...) custom-call(s32[2,128]{1,0:T(2,128)S(1)} %bitcast.3, bf16[2,128]{1,0:T(2,128)(2,1)S(1)} %bitcast.4, ...), custom_call_target="tpu_custom_call" | custom-call | tf_op jit(solution)/shard_map/route_and_forward/pallas_call | solution.py:323
  37.2 6.7 %outer_products.1 = (bf16[1,448,4096]{2,1,0:T(8,128)(2,1)}, bf16[1,448,4096]{2,1,0:T(8,128)(2,1)}, bf16[1,448,4096]{2,1,0:T(8,128)(2,1)}, f32[2,128]{1,0:T(2,128)}) custom-call(bf16[256,1024]{1,0:T(8,128)(2,1)S(1)} %get-tuple-element.14.x_ref, bf16[256,1024]{1,0:T(8,128)(2,1)S(1)} %get-tuple-element.15.sdy_ref, ...), custom_call_target="tpu_custom_call" | custom-call | tf_op jit(solution)/shard_map/outer_products/pallas_call | solution.py:367
Async XLA Ops:
  0.6 1.2 %copy-start = (bf16[128,4096]{1,0:T(8,128)(2,1)S(1)}, bf16[128,4096]{1,0:T(8,128)(2,1)}, u32[]{:S(2)}) copy-start(bf16[128,4096]{1,0:T(8,128)(2,1)} %tok_hbm.1) | copy-start | bytes 3145732
  1.9 1.2 %copy-start.1 = (bf16[128,4096]{1,0:T(8,128)(2,1)S(1)}, bf16[128,4096]{1,0:T(8,128)(2,1)}, u32[]{:S(2)}) copy-start(bf16[128,4096]{1,0:T(8,128)(2,1)} %cot_hbm.1) | copy-start | bytes 3145732
  3.1 0.7 %copy-start.2 = (s32[128,2]{0,1:T(2,128)S(1)}, s32[128,2]{0,1:T(2,128)}, u32[]{:S(2)}) copy-start(s32[128,2]{0,1:T(2,128)} %param.9) | copy-start | bytes 3076
  3.8 0.7 %copy-start.3 = (bf16[128,2]{0,1:T(2,128)(2,1)S(1)}, bf16[128,2]{0,1:T(2,128)(2,1)}, u32[]{:S(2)}) copy-start(bf16[128,2]{0,1:T(2,128)(2,1)} %param.10) | copy-start | bytes 1540

commit v4 on v3

--- a/solution.py
+++ b/solution.py
@@ -25,9 +25,9 @@
 
 def forward_kernel(
     n_dp, n_e, recv,
-    ids_ref, prob_ref, tok_hbm, cot_hbm, gate_hbm, up_hbm, down_hbm,
+    ids_hbm, prob_hbm, tok_hbm, cot_hbm, gate_hbm, up_hbm, down_hbm,
     x_out, sdy_out, dg_out, du_out, hid_out, gp_out,
-    tok, cot, wg, wu, wd, sx, sd, yx, yd, gx, gd, pre_g, pre_u, rbuf,
+    ids_ref, prob_ref, tok, cot, wg, wu, wd, sx, sd, yx, yd, gx, gd, pre_g, pre_u, rbuf,
     load_sem, y_send, y_recv, z_send, mid_send, core_send, g_recv, r_send, r_recv,
 ):
     me = lax.axis_index("dp")
@@ -45,22 +45,34 @@
         pltpu.make_async_copy(src, dst, load_sem.at[k])
         for k, (src, dst) in enumerate(
             ((tok_hbm, tok), (cot_hbm, cot), (gate_hbm.at[0], wg), (up_hbm.at[0], wu),
-             (down_hbm.at[0], wd))
+             (down_hbm.at[0], wd), (ids_hbm, ids_ref), (prob_hbm, prob_ref))
         )
     ]
-    for load in loads:
+    for load in loads[5:] + loads[:5]:
         load.start()
 
     barrier = pltpu.get_barrier_semaphore()
     n_all = n_dp * n_e
-    flat = me * n_e + ex
-
-    def greet(o, carry):
-        to = (flat + o) % n_all
-        pl.semaphore_signal(barrier, inc=1, device_id=(to // n_e, to % n_e), device_id_type=MESH)
-        return carry
-
-    lax.fori_loop(1, n_all, greet, 0)
+
+    def each(act):
+        def step(o, skip):
+            to = me + o
+            to = jnp.where(to >= n_dp, to - n_dp, to)
+            for f in range(skip, n_e):
+                there = ex + f
+                act(o, f, (to, jnp.where(there >= n_e, there - n_e, there)))
+
+        step(0, 1)
+        if n_all <= 32:
+            for o in range(1, n_dp):
+                step(o, 0)
+        else:
+            lax.fori_loop(1, n_dp, lambda o, carry: (step(o, 0), carry)[1], 0)
+
+    each(lambda o, f, to: pl.semaphore_signal(
+        barrier, inc=1, device_id=to, device_id_type=MESH))
+    loads[5].wait()
+    loads[6].wait()
 
     id0, id1 = ids_ref[0:1, :], ids_ref[1:2, :]
     p0, p1 = prob_ref[0:1, :].astype(F32), prob_ref[1:2, :].astype(F32)
@@ -236,19 +248,13 @@
     hidden = (silu * up_pre).astype(BF16)
     rbuf[ex, me] = jnp.sum(hidden.astype(F32) * pulled, axis=0, keepdims=True)
 
-    def router_copy(o, slot):
-        to = (flat + o) % n_all
-        there = ex if slot else to % n_e, me if slot else to // n_e
+    def router_copy(o, f, device, slot):
         return pltpu.make_async_remote_copy(
-            src_ref=rbuf.at[there], dst_ref=rbuf.at[there],
-            send_sem=r_send.at[o], recv_sem=r_recv.at[there],
-            device_id=(to // n_e, to % n_e), device_id_type=MESH)
-
-    def send_router(o, carry):
-        router_copy(o, True).start()
-        return carry
-
-    lax.fori_loop(1, n_all, send_router, 0)
+            src_ref=rbuf.at[slot[1], slot[0]], dst_ref=rbuf.at[slot[1], slot[0]],
+            send_sem=r_send.at[f, o], recv_sem=r_recv.at[slot[1], slot[0]],
+            device_id=device, device_id_type=MESH)
+
+    each(lambda o, f, to: router_copy(o, f, to, (me, ex)).start())
 
     hid_out[...] = hidden
     d_hidden = p_row * pulled
@@ -266,11 +272,7 @@
             for m in range(mid_n):
                 core_copy(k, l, m).wait_send()
 
-    def get_router(o, carry):
-        router_copy(o, False).wait_recv()
-        return carry
-
-    lax.fori_loop(1, n_all, get_router, 0)
+    each(lambda o, f, to: router_copy(o, f, to, to).wait_recv())
 
     before = jnp.zeros((1, 128), F32)
     for e in range(n_e):
@@ -286,26 +288,34 @@
     gp_out[0:1, :] = jnp.sum(jnp.where(first, found, 0.0), axis=0, keepdims=True)
     gp_out[1:2, :] = jnp.sum(jnp.where(second, found, 0.0), axis=0, keepdims=True)
 
-    def sent_router(o, carry):
-        router_copy(o, True).wait_send()
-        return carry
-
-    lax.fori_loop(1, n_all, sent_router, 0)
-
-
-def grads_kernel(recv, per_piece, x_ref, sdy_ref, dg_ref, du_ref, hid_ref, gp_ref,
-                 gg_ref, gu_ref, gd_ref, gp_out):
-    piece = pl.program_id(0) // per_piece
-    keep = (iota(dg_ref.shape, 1) % BLOCK) // recv == piece
-
-    def outer(d_ref, rows_ref, out_ref):
-        d = jnp.where(keep, d_ref[...].astype(F32), 0.0).astype(BF16)
-        out_ref[0] = jnp.dot(d, rows_ref[...], preferred_element_type=F32).astype(BF16)
-
-    outer(dg_ref, x_ref, gg_ref)
-    outer(du_ref, x_ref, gu_ref)
-    outer(hid_ref, sdy_ref, gd_ref)
+    each(lambda o, f, to: router_copy(o, f, to, (me, ex)).wait_send())
+
+
+def grads_kernel(
+    recv, tile, x_ref, sdy_ref, dg_ref, du_ref, hid_ref, gp_ref, gg_hbm, gu_hbm, gd_hbm, gp_out,
+    stage, sems,
+):
+    pieces = BLOCK // recv
+    per_piece = x_ref.shape[1] // tile
+    piece_of = (iota(dg_ref.shape, 1) % BLOCK) // recv
+    copies = []
+    for piece in range(pieces):
+        for k, (d_ref, rows_ref, out_hbm) in enumerate(
+            ((dg_ref, x_ref, gg_hbm), (du_ref, x_ref, gu_hbm), (hid_ref, sdy_ref, gd_hbm))
+        ):
+            d = jnp.where(piece_of == piece, d_ref[...].astype(F32), 0.0).astype(BF16)
+            for part in range(per_piece):
+                b = piece * per_piece + part
+                stage[k, b] = jnp.dot(
+                    d, rows_ref[:, part * tile:(part + 1) * tile], preferred_element_type=F32
+                ).astype(BF16)
+                copy = pltpu.make_async_copy(
+                    stage.at[k, b], out_hbm.at[0, :, pl.ds(b * tile, tile)], sems.at[k, b])
+                copy.start()
+                copies.append(copy)
     gp_out[...] = gp_ref[...]
+    for copy in copies:
+        copy.wait()
 
 
 def shards(n_dp, n_e, tokens, cotangent, expert_ids, gate_probs, gate_w, up_w, down_w):
@@ -330,9 +340,11 @@
             jax.ShapeDtypeStruct((hidden_n, n_rows), BF16),
             jax.ShapeDtypeStruct((2, n_t), F32),
         ),
-        in_specs=[vmem, vmem] + [hbm] * 5,
+        in_specs=[hbm] * 7,
         out_specs=[vmem] * 6,
         scratch_shapes=[
+            pltpu.VMEM((2, n_t), jnp.int32),
+            pltpu.VMEM((2, n_t), BF16),
             pltpu.VMEM((n_t, width), BF16),
             pltpu.VMEM((n_t, width), BF16),
             pltpu.VMEM((hidden_n, width), BF16),
@@ -347,29 +359,29 @@
             pltpu.VMEM((hidden_n, n_rows), F32),
             pltpu.VMEM((hidden_n, n_rows), F32),
             pltpu.VMEM((n_e, n_dp, 1, n_rows), F32),
-            dma((5,)),
+            dma((7,)),
             dma((2, n_e)), dma((2, n_e)),
             dma((2, LINE)), dma((2, mid_n, LINE)), dma((2, LINE, mid_n)), dma((2, n_dp)),
-            dma((n_dp * n_e,)), dma((n_e, n_dp)),
+            dma((n_e, n_dp)), dma((n_e, n_dp)),
         ],
         compiler_params=pltpu.CompilerParams(
             collective_id=0, has_side_effects=True, vmem_limit_bytes=48 * 1024 * 1024),
         name="route_and_forward",
-    )(expert_ids.T, gate_probs.T, tokens, cotangent, gate_w, up_w, down_w)
+    )(*(
+        pltpu.with_memory_space_constraint(v, pltpu.HBM)
+        for v in (expert_ids.T, gate_probs.T, tokens, cotangent, gate_w, up_w, down_w)))
 
     tile = 512
-    per_piece = cols // tile
-    whole = pl.BlockSpec((hidden_n, n_rows), lambda b: (0, 0))
-    part = pl.BlockSpec((n_rows, tile), lambda b: (0, b % per_piece))
     grad = jax.ShapeDtypeStruct((1, hidden_n, width), BF16)
-    out = pl.BlockSpec((1, hidden_n, tile), lambda b: (0, 0, b))
-    small = pl.BlockSpec((2, n_t), lambda b: (0, 0))
     gg, gu, gd, gp = pl.pallas_call(
-        functools.partial(grads_kernel, recv, per_piece),
-        grid=(width // tile,),
+        functools.partial(grads_kernel, recv, tile),
         out_shape=(grad, grad, grad, jax.ShapeDtypeStruct((2, n_t), F32)),
-        in_specs=[part, part, whole, whole, whole, small],
-        out_specs=[out, out, out, small],
+        in_specs=[vmem] * 6,
+        out_specs=[hbm] * 3 + [vmem],
+        scratch_shapes=[
+            pltpu.VMEM((3, width // tile, hidden_n, tile), BF16),
+            dma((3, width // tile)),
+        ],
         compiler_params=pltpu.CompilerParams(vmem_limit_bytes=32 * 1024 * 1024),
         name="outer_products",
     )(x, sdy, dg, du, hid, gp)

time: 44 us -> 37.8 us (0.86)
  local copies, waits for them, and re-layouts: 3.78 us -> 0 us
  Pallas kernels: 39.4 us -> 37 us
    unnamed x8 -> x0, local copies, waits for them, and re-layouts: 3.78 us -> none
    pallas_call x1, Pallas kernels: 6.66 us -> 5.13 us  [shards(): pl.pallas_call(functools.partial(grads_kernel, recv, tile), out_shape=(gr...]
    pallas_call x1, Pallas kernels: 32.7 us -> 31.9 us  [shards(): pl.pallas_call(functools.partial(forward_kernel, n_dp, n_e, recv), out_sh...]
where the time goes in v4:
time: 37.8 us; the launch traced here: 37.7 us
  Pallas kernels  37 us (98%)
  between operations  0.64 us (2%)
    pallas_call x1, Pallas kernels, shards(): pl.pallas_call(functools.partial(forward_kernel, n_dp, n_e, recv), out_sh...  31.9 us
    pallas_call x1, Pallas kernels, shards(): pl.pallas_call(functools.partial(grads_kernel, recv, tile), out_shape=(gr...  5.13 us

profile of v4, /device:TPU:0, one launch (start us, length us, event | category | flops | bytes accessed | tf_op | source)
XLA Modules:
  0.0 37.7 jit_solution(6917408111963342457)
XLA Ops:
  0.6 31.9 %route_and_forward.1 = (bf16[256,1024]{1,0:T(8,128)(2,1)S(1)}, bf16[256,1024]{1,0:T(8,128)(2,1)S(1)}, bf16[448,256]{1,0:T(8,128)(2,1)S(1)}, bf16[448,256]{1,0:T(...) custom-call(s32[2,128]{1,0:T(2,128)} %bitcast.3, bf16[2,128]{1,0:T(2,128)(2,1)} %bitcast.4, ...), custom_call_target="tpu_custom_call" | custom-call | tf_op jit(solution)/shard_map/route_and_forward/pallas_call | solution.py:333
  32.5 5.1 %outer_products.1 = (bf16[1,448,4096]{2,1,0:T(8,128)(2,1)}, bf16[1,448,4096]{2,1,0:T(8,128)(2,1)}, bf16[1,448,4096]{2,1,0:T(8,128)(2,1)}, f32[2,128]{1,0:T(2,128)}) custom-call(bf16[256,1024]{1,0:T(8,128)(2,1)S(1)} %get-tuple-element.14.x_ref, bf16[256,1024]{1,0:T(8,128)(2,1)S(1)} %get-tuple-element.15.sdy_ref, ...), custom_call_target="tpu_custom_call" | custom-call | tf_op jit(solution)/shard_map/outer_products/pallas_call | solution.py:376

commit v5 on v4

--- a/solution.py
+++ b/solution.py
@@ -23,10 +23,18 @@
     return lax.dot_general(a, b, (((1,), (1,)), ((), ())), preferred_element_type=F32)
 
 
+def outer_tile(recv, tile, b, d_ref, rows_ref):
+    per_piece = rows_ref.shape[1] // tile
+    keep = (iota(d_ref.shape, 1) % BLOCK) // recv == b // per_piece
+    d = jnp.where(keep, d_ref[...].astype(F32), 0.0).astype(BF16)
+    at = b % per_piece * tile
+    return jnp.dot(d, rows_ref[:, at:at + tile], preferred_element_type=F32).astype(BF16)
+
+
 def forward_kernel(
     n_dp, n_e, recv,
     ids_hbm, prob_hbm, tok_hbm, cot_hbm, gate_hbm, up_hbm, down_hbm,
-    x_out, sdy_out, dg_out, du_out, hid_out, gp_out,
+    x_out, sdy_out, dg_out, du_out, hid_out, gp_out, early_out,
     ids_ref, prob_ref, tok, cot, wg, wu, wd, sx, sd, yx, yd, gx, gd, pre_g, pre_u, rbuf,
     load_sem, y_send, y_recv, z_send, mid_send, core_send, g_recv, r_send, r_recv,
 ):
@@ -48,7 +56,7 @@
              (down_hbm.at[0], wd), (ids_hbm, ids_ref), (prob_hbm, prob_ref))
         )
     ]
-    for load in loads[5:] + loads[:5]:
+    for load in loads[5:] + loads[:2]:
         load.start()
 
     barrier = pltpu.get_barrier_semaphore()
@@ -115,6 +123,8 @@
         y_copy(0, e, ex).start()
     yx[ex] = sx[ex]
     loads[1].wait()
+    for load in loads[2:5]:
+        load.start()
     sd[...] = gather(cot).reshape(n_e, BLOCK, cols)
     for e in others:
         y_copy(1, e, ex).start()
@@ -261,6 +271,13 @@
     dg_out[...] = (d_hidden * up_pre * sigma * (1.0 + gate_pre * (1.0 - sigma))).astype(BF16)
     du_out[...] = (d_hidden * silu).astype(BF16)
 
+    half, tile = early_out.shape[1], early_out.shape[3]
+    for k, (d_ref, rows_ref) in enumerate(
+        ((dg_out, x_out), (du_out, x_out), (hid_out, sdy_out))
+    ):
+        for tile_no in range(half):
+            early_out[k, tile_no] = outer_tile(recv, tile, tile_no, d_ref, rows_ref)
+
     for k in range(2):
         for e in others:
             y_copy(k, e, ex).wait_send()
@@ -292,27 +309,28 @@
 
 
 def grads_kernel(
-    recv, tile, x_ref, sdy_ref, dg_ref, du_ref, hid_ref, gp_ref, gg_hbm, gu_hbm, gd_hbm, gp_out,
-    stage, sems,
+    recv, x_ref, sdy_ref, dg_ref, du_ref, hid_ref, gp_ref, early_ref, gg_hbm, gu_hbm, gd_hbm,
+    gp_out, stage, sems,
 ):
-    pieces = BLOCK // recv
-    per_piece = x_ref.shape[1] // tile
-    piece_of = (iota(dg_ref.shape, 1) % BLOCK) // recv
+    half, tile = early_ref.shape[1], early_ref.shape[3]
+    outs = (gg_hbm, gu_hbm, gd_hbm)
     copies = []
-    for piece in range(pieces):
-        for k, (d_ref, rows_ref, out_hbm) in enumerate(
-            ((dg_ref, x_ref, gg_hbm), (du_ref, x_ref, gu_hbm), (hid_ref, sdy_ref, gd_hbm))
+
+    def leave(src, k, b):
+        copy = pltpu.make_async_copy(
+            src, outs[k].at[0, :, pl.ds(b * tile, tile)], sems.at[k, b])
+        copy.start()
+        copies.append(copy)
+
+    for b in range(half):
+        for k in range(3):
+            leave(early_ref.at[k, b], k, b)
+    for b in range(half, sems.shape[1]):
+        for k, (d_ref, rows_ref) in enumerate(
+            ((dg_ref, x_ref), (du_ref, x_ref), (hid_ref, sdy_ref))
         ):
-            d = jnp.where(piece_of == piece, d_ref[...].astype(F32), 0.0).astype(BF16)
-            for part in range(per_piece):
-                b = piece * per_piece + part
-                stage[k, b] = jnp.dot(
-                    d, rows_ref[:, part * tile:(part + 1) * tile], preferred_element_type=F32
-                ).astype(BF16)
-                copy = pltpu.make_async_copy(
-                    stage.at[k, b], out_hbm.at[0, :, pl.ds(b * tile, tile)], sems.at[k, b])
-                copy.start()
-                copies.append(copy)
+            stage[k, b - half] = outer_tile(recv, tile, b, d_ref, rows_ref)
+            leave(stage.at[k, b - half], k, b)
     gp_out[...] = gp_ref[...]
     for copy in copies:
         copy.wait()
@@ -330,7 +348,9 @@
     hbm = pl.BlockSpec(memory_space=pltpu.HBM)
     vmem = pl.BlockSpec(memory_space=pltpu.VMEM)
     dma = pltpu.SemaphoreType.DMA
-    x, sdy, dg, du, hid, gp = pl.pallas_call(
+    tile = 512
+    half = width // tile // 2
+    x, sdy, dg, du, hid, gp, early = pl.pallas_call(
         functools.partial(forward_kernel, n_dp, n_e, recv),
         out_shape=(
             jax.ShapeDtypeStruct((n_rows, cols), BF16),
@@ -339,9 +359,10 @@
             jax.ShapeDtypeStruct((hidden_n, n_rows), BF16),
             jax.ShapeDtypeStruct((hidden_n, n_rows), BF16),
             jax.ShapeDtypeStruct((2, n_t), F32),
+            jax.ShapeDtypeStruct((3, half, hidden_n, tile), BF16),
         ),
         in_specs=[hbm] * 7,
-        out_specs=[vmem] * 6,
+        out_specs=[vmem] * 7,
         scratch_shapes=[
             pltpu.VMEM((2, n_t), jnp.int32),
             pltpu.VMEM((2, n_t), BF16),
@@ -365,26 +386,25 @@
             dma((n_e, n_dp)), dma((n_e, n_dp)),
         ],
         compiler_params=pltpu.CompilerParams(
-            collective_id=0, has_side_effects=True, vmem_limit_bytes=48 * 1024 * 1024),
+            collective_id=0, has_side_effects=True, vmem_limit_bytes=40 * 1024 * 1024),
         name="route_and_forward",
     )(*(
         pltpu.with_memory_space_constraint(v, pltpu.HBM)
         for v in (expert_ids.T, gate_probs.T, tokens, cotangent, gate_w, up_w, down_w)))
 
-    tile = 512
     grad = jax.ShapeDtypeStruct((1, hidden_n, width), BF16)
     gg, gu, gd, gp = pl.pallas_call(
-        functools.partial(grads_kernel, recv, tile),
+        functools.partial(grads_kernel, recv),
         out_shape=(grad, grad, grad, jax.ShapeDtypeStruct((2, n_t), F32)),
-        in_specs=[vmem] * 6,
+        in_specs=[vmem] * 7,
         out_specs=[hbm] * 3 + [vmem],
         scratch_shapes=[
-            pltpu.VMEM((3, width // tile, hidden_n, tile), BF16),
+            pltpu.VMEM((3, width // tile - half, hidden_n, tile), BF16),
             dma((3, width // tile)),
         ],
         compiler_params=pltpu.CompilerParams(vmem_limit_bytes=32 * 1024 * 1024),
         name="outer_products",
-    )(x, sdy, dg, du, hid, gp)
+    )(x, sdy, dg, du, hid, gp, early)
     return gg, gu, gd, gp.T
 
 

time: 37.8 us -> 37.5 us (level)
  no operation moved by 1% of the time
where the time goes in v5:
time: 37.5 us; the launch traced here: 37.3 us
  Pallas kernels  36.7 us (98%)
  between operations  0.64 us (2%)
    pallas_call x1, Pallas kernels, shards(): pl.pallas_call(functools.partial(forward_kernel, n_dp, n_e, recv), out_sh...  31.8 us
    pallas_call x1, Pallas kernels, shards(): pl.pallas_call(functools.partial(grads_kernel, recv), out_shape=(grad, gr...  4.89 us

profile of v5, /device:TPU:0, one launch (start us, length us, event | category | flops | bytes accessed | tf_op | source)
XLA Modules:
  0.0 37.3 jit_solution(9495619199645310842)
XLA Ops:
  0.6 31.8 %route_and_forward.1 = (bf16[256,1024]{1,0:T(8,128)(2,1)S(1)}, bf16[256,1024]{1,0:T(8,128)(2,1)S(1)}, bf16[448,256]{1,0:T(8,128)(2,1)S(1)}, bf16[448,256]{1,0:T(...) custom-call(s32[2,128]{1,0:T(2,128)} %bitcast.3, ...), custom_call_target="tpu_custom_call" | custom-call | tf_op jit(solution)/shard_map/route_and_forward/pallas_call | solution.py:353
  32.5 4.9 %outer_products.1 = (bf16[1,448,4096]{2,1,0:T(8,128)(2,1)}, bf16[1,448,4096]{2,1,0:T(8,128)(2,1)}, bf16[1,448,4096]{2,1,0:T(8,128)(2,1)}, f32[2,128]{1,0:T(2,128)}) custom-call(bf16[256,1024]{1,0:T(8,128)(2,1)S(1)} %get-tuple-element.15.x_ref, bf16[256,1024]{1,0:T(8,128)(2,1)S(1)} %get-tuple-element.16.sdy_ref, ...), custom_call_target="tpu_custom_call" | custom-call | tf_op jit(solution)/shard_map/outer_products/pallas_call | solution.py:396
